TPU v7x, 256 devices: a whole 4x4x8 slice. The times are simulated.
256 devices in a mesh: row: 32 (over y, x, core), col: 8 (over z).
Axes of the slice: x: 4, y: 4, z: 8, core: 2. Of those that a mesh axis runs over, the one named last changes fastest.
Arguments:
- block_values: bfloat16 [32, 8, 128, 128, 128], P('row', 'col'), may hold values from -50 to 50
- block_index: int32 [32, 8, 2, 128], P('row', 'col'), may hold values from 0 to 255, as said below
- block_count: int32 [32, 8], P('row', 'col'), may hold values from 1 to 128
- start_vectors: float32 [32768, 256], P(('row', 'col')), may hold values from -40 to 40
Outputs:
- basis: float32 [32768, 256], P(('row', 'col'))
- projected: float32 [256, 256], replicated
- ritz_residual: float32 [32768, 256], P(('row', 'col'))
- gram_scaled: float32 [256, 256], replicated
Inputs may be any that keep to these rules, and one draw needn't show every extreme that they name: Every slot of the device at row index r and col index c holds a pair (i, j) = (block_index[r, c, 0, s], block_index[r, c, 1, s]) with i // 8 = r and j % 8 = c. The slots below block_count[r, c] hold distinct blocks with i <= j; the later slots hold pairs that are not part of the matrix.
All inputs are finite; a program needn't handle non-finite values.
Results may differ from a plain program's by a relative error of at most 0.0051.
Values may be sent and summed in bfloat16 or wider, within the bound.
A program may use at most 128 MiB of HBM per device.

v0:
```python
import math

import jax
import jax.numpy as jnp
from jax import lax
from jax.sharding import PartitionSpec as P

ITERS = 2


slot_group = 8
highest = lax.Precision.HIGHEST


def local_products(blocks, first_ids, second_ids, live_count, row_slab, col_slab, row_acc, col_acc):
    col_devices = row_slab.shape[0]

    def group_step(group_index, accums):
        row_part, col_part = accums
        first_slot = group_index * slot_group
        pieces = lax.dynamic_slice_in_dim(blocks, first_slot, slot_group, 0)
        row_ids = lax.dynamic_slice_in_dim(first_ids, first_slot, slot_group, 0) % col_devices
        col_ids = lax.dynamic_slice_in_dim(second_ids, first_slot, slot_group, 0) // col_devices
        live_mask = (first_slot + jnp.arange(slot_group, dtype=jnp.int32) < live_count)[
            :, None, None
        ]
        ahead = jnp.einsum(
            "gab,gbk->gak", pieces, col_slab[col_ids], preferred_element_type=jnp.float32
        )
        ahead = jnp.where(live_mask, ahead, 0.0)
        row_part = row_part.at[row_ids].add(ahead)
        behind = jnp.einsum(
            "gba,gbk->gak", pieces, row_slab[row_ids], preferred_element_type=jnp.float32
        )
        behind = jnp.where(live_mask, behind, 0.0)
        col_part = col_part.at[col_ids].add(behind)
        return (row_part, col_part)

    group_count = (live_count + slot_group - 1) // slot_group
    return lax.fori_loop(0, group_count, group_step, (row_acc, col_acc))


def orthonormal(tall_block):
    local_gram = jnp.einsum("nk,nm->km", tall_block, tall_block, precision=highest)
    gram_sum = lax.psum(local_gram, ("row", "col"))
    factor = jnp.linalg.cholesky(gram_sum)
    return (jax.scipy.linalg.solve_triangular(factor, tall_block.T, lower=True).T, gram_sum)


def local(block_values, block_index, block_count, start_vectors):
    row_devices = lax.axis_size("row")
    col_devices = lax.axis_size("col")
    blocks = block_values[0, 0]
    own_index = block_index[0, 0]
    live_count = block_count[0, 0]
    slot_total = blocks.shape[0]
    block_size = blocks.shape[1]
    vec_width = start_vectors.shape[1]
    first_ids = own_index[0]
    second_ids = own_index[1]
    live_flags = jnp.arange(slot_total, dtype=jnp.int32) < live_count
    live_mask = live_flags.astype(jnp.float32)[:, None]
    magnitude = jnp.abs(blocks)
    across = jnp.sum(magnitude, axis=2, dtype=jnp.float32) * live_mask
    downward = jnp.sum(magnitude, axis=1, dtype=jnp.float32) * live_mask
    row_sums = (
        jnp.zeros((col_devices, block_size), jnp.float32).at[first_ids % col_devices].add(across)
    )
    col_sums = (
        jnp.zeros((row_devices, block_size), jnp.float32)
        .at[second_ids // col_devices]
        .add(downward)
    )
    degree = lax.psum_scatter(row_sums, "col", scatter_dimension=0, tiled=True) + lax.psum_scatter(
        col_sums, "row", scatter_dimension=0, tiled=True
    )
    inverse_root = (1.0 / jnp.sqrt(degree / block_size + 1e-05)).reshape(block_size, 1)

    def apply_operator(vectors):
        weighted = (inverse_root * vectors).astype(jnp.bfloat16)
        row_slab = lax.all_gather(weighted, "col", axis=0, tiled=True).reshape(
            col_devices, block_size, vec_width
        )
        col_slab = lax.all_gather(weighted, "row", axis=0, tiled=True).reshape(
            row_devices, block_size, vec_width
        )
        row_acc = jnp.zeros((col_devices, block_size, vec_width), jnp.float32)
        col_acc = jnp.zeros((row_devices, block_size, vec_width), jnp.float32)
        row_acc, col_acc = local_products(
            blocks, first_ids, second_ids, live_count, row_slab, col_slab, row_acc, col_acc
        )
        own_rows = lax.psum_scatter(
            row_acc.reshape(col_devices * block_size, vec_width),
            "col",
            scatter_dimension=0,
            tiled=True,
        )
        own_cols = lax.psum_scatter(
            col_acc.reshape(row_devices * block_size, vec_width),
            "row",
            scatter_dimension=0,
            tiled=True,
        )
        return inverse_root * (own_rows + own_cols)

    subspace = start_vectors
    last_gram = jnp.zeros((vec_width, vec_width), jnp.float32)
    for iteration in range(ITERS):
        subspace, last_gram = orthonormal(apply_operator(subspace))
    gram_scaled = last_gram / jnp.sqrt(jnp.mean(last_gram * last_gram) + 1e-06)
    mapped = apply_operator(subspace)
    local_ritz = jnp.einsum("nk,nm->km", subspace, mapped, precision=highest)
    ritz = lax.psum(local_ritz, ("row", "col"))
    spread = jnp.sqrt(jnp.mean(ritz * ritz) + 1e-06)
    total_rows = block_size * row_devices * col_devices
    residual = (mapped - jnp.dot(subspace, ritz, precision=highest)) * (
        math.sqrt(total_rows / vec_width) / spread
    )
    return (subspace * math.sqrt(total_rows), ritz / spread, residual, gram_scaled)


def solution(mesh):
    return jax.shard_map(
        local,
        mesh=mesh,
        in_specs=(
            P("row", "col", None, None, None),
            P("row", "col", None, None),
            P("row", "col"),
            P(("row", "col"), None),
        ),
        out_specs=(P(("row", "col"), None), P(), P(("row", "col"), None), P()),
        check_vma=False,
    )
```

profile of v0, /device:TPU:1, one launch (start us, length us, event | category | flops | bytes accessed | tf_op | source)
XLA Modules:
  0.0 2126.8 jit_solution(14992519715849911646)
XLA Ops:
  8.0 3.7 convert_reduce_fusion.1
  12.7 124.2 %all-reduce.2 = f32[32,128]{1,0:T(8,128)S(1)} all-reduce(f32[32,128]{1,0:T(8,128)S(1)} %scatter_custom_fusion.7), channel_id=3, replica_groups=mesh['row'=32,'col'=8] {'row'}, use_global_device_ids=true, to_apply=%region_5.6.clone | all-reduce | flops 4096 | bytes 32768
  138.3 16.3 all-reduce.1
  157.9 19.4 all_gather.19
  177.2 31.7 %all-gather.4.cloned.1.call-done = bf16[4096,256]{1,0:T(8,128)(2,1)} async-done(((bf16[128,256]{1,0:T(8,128)(2,1)}), bf16[4096,256]{1,0:T(8,128)(2,1)}) %all-gather.4.cloned.1.call-update) | async-done | bytes 2097168 | tf_op jit(solution)/shard_map/all_gather | solution.py:84
  211.5 107.6 %while.46 = (s32[]{:T(128)}, f32[8,128,256]{2,1,0:T(8,128)S(1)}, f32[32,128,256]{2,1,0:T(8,128)}, s32[]{:T(128)}, s32[128]{0:T(128)S(1)}, /*index=5*/s32[]{:T(12...) while((s32[]{:T(128)}, f32[8,128,256]{2,1,0:T(8,128)S(1)}, ...), condition=%wide.region_9.10_spmd, body=%wide.region_6.9_spmd.sunk | while | flops 135268640 | bytes 12067359 | solution.py:40
  214.2 3.3 scatter_fusion.1
  224.9 3.4 scatter_fusion.1
  246.5 3.3 scatter_fusion.1
  278.7 3.4 scatter_fusion.1
  310.9 3.3 scatter_fusion.1
  320.9 92.3 %reduce-scatter.7.cloned.1.call-done = f32[128,256]{1,0:T(8,128)} async-done(((f32[1024,256]{1,0:T(8,128)}), f32[128,256]{1,0:T(8,128)}) %reduce-scatter.7.cloned.1.call-update) | async-done | bytes 131088 | tf_op jit(solution)/shard_map/reduce_scatter | solution.py:92
  413.2 95.1 %reduce-scatter.9.cloned.1.call-done = f32[128,256]{1,0:T(8,128)} async-done(((f32[4096,256]{1,0:T(8,128)}), f32[128,256]{1,0:T(8,128)}) %reduce-scatter.9.cloned.1.call-update) | async-done | bytes 131088 | tf_op jit(solution)/shard_map/reduce_scatter | solution.py:98
  512.0 253.0 %all-reduce.7.cloned.1.call-done = f32[256,256]{0,1:T(8,128)} async-done(((f32[256,256]{0,1:T(8,128)}), f32[256,256]{0,1:T(8,128)}) %all-reduce.7.cloned.1.call-update) | async-done | bytes 262160 | tf_op jit(solution)/shard_map/psum | solution.py:45
  767.1 11.7 cholesky.130
  778.9 9.8 custom-call.13
  789.2 11.7 cholesky.147
  803.0 4.5 while.49
  807.5 19.7 custom-call.14
  828.8 21.9 %all_gather.21 = bf16[1024,256]{0,1:T(8,128)(2,1)S(1)} all-gather(bf16[128,256]{0,1:T(8,128)(2,1)} %fusion.20), channel_id=1, replica_groups=mesh['row'=32,'col'=8] {'col'}, dimensions={0}, use_global_device_ids=true | all-gather | bytes 589824 | tf_op jit(solution)/shard_map/all_gather | solution.py:81
  850.9 28.3 %all-gather.6.cloned.1.call-done = bf16[4096,256]{0,1:T(8,128)(2,1)} async-done(((bf16[128,256]{0,1:T(8,128)(2,1)}), bf16[4096,256]{0,1:T(8,128)(2,1)}) %all-gather.6.cloned.1.call-update) | async-done | bytes 2097168 | tf_op jit(solution)/shard_map/all_gather | solution.py:84
  879.2 4.1 copy.39
  885.8 107.6 %while.47 = (s32[]{:T(128)}, f32[8,128,256]{2,1,0:T(8,128)S(1)}, f32[32,128,256]{2,1,0:T(8,128)}, s32[]{:T(128)}, s32[128]{0:T(128)S(1)}, /*index=5*/s32[]{:T(12...) while((s32[]{:T(128)}, f32[8,128,256]{2,1,0:T(8,128)S(1)}, ...), condition=%wide.region_20.23_spmd, body=%wide.region_17.22_spmd.sunk | while | flops 135268640 | bytes 12067359 | solution.py:40
  888.4 3.3 scatter_fusion.3
  899.2 3.4 scatter_fusion.3
  920.8 3.3 scatter_fusion.3
  953.0 3.4 scatter_fusion.3
  985.2 3.3 scatter_fusion.3
  995.2 91.9 %reduce-scatter.11.cloned.1.call-done = f32[128,256]{1,0:T(8,128)} async-done(((f32[1024,256]{1,0:T(8,128)}), f32[128,256]{1,0:T(8,128)}) %reduce-scatter.11.cloned.1.call-update) | async-done | bytes 131088 | tf_op jit(solution)/shard_map/reduce_scatter | solution.py:92
  1087.1 96.1 %reduce-scatter.13.cloned.1.call-done = f32[128,256]{1,0:T(8,128)} async-done(((f32[4096,256]{1,0:T(8,128)}), f32[128,256]{1,0:T(8,128)}) %reduce-scatter.13.cloned.1.call-update) | async-done | bytes 131088 | tf_op jit(solution)/shard_map/reduce_scatter | solution.py:98
  1186.8 252.3 %all-reduce.9.cloned.1.call-done = f32[256,256]{0,1:T(8,128)} async-done(((f32[256,256]{0,1:T(8,128)}), f32[256,256]{0,1:T(8,128)}) %all-reduce.9.cloned.1.call-update) | async-done | bytes 262160 | tf_op jit(solution)/shard_map/psum | solution.py:45
  1441.2 11.7 cholesky.164
  1452.9 9.8 custom-call.15
  1463.2 11.7 cholesky.181
  1477.6 4.2 while.50
  1481.8 19.7 custom-call.16
  1503.1 21.9 %all_gather.23 = bf16[1024,256]{0,1:T(8,128)(2,1)S(1)} all-gather(bf16[128,256]{0,1:T(8,128)(2,1)} %get-tuple-element.560), channel_id=1, replica_groups=mesh['row'=32,'col'=8] {'col'}, dimensions={0}, use_global_device_ids=true | all-gather | bytes 589824 | tf_op jit(solution)/shard_map/all_gather | solution.py:81
  1525.2 28.3 %all-gather.8.cloned.1.call-done = bf16[4096,256]{0,1:T(8,128)(2,1)} async-done(((bf16[128,256]{0,1:T(8,128)(2,1)}), bf16[4096,256]{0,1:T(8,128)(2,1)}) %all-gather.8.cloned.1.call-update) | async-done | bytes 2097168 | tf_op jit(solution)/shard_map/all_gather | solution.py:84
  1553.5 4.1 copy.41
  1560.1 107.6 %while.48 = (s32[]{:T(128)}, f32[8,128,256]{2,1,0:T(8,128)S(1)}, f32[32,128,256]{2,1,0:T(8,128)}, s32[]{:T(128)}, s32[128]{0:T(128)S(1)}, /*index=5*/s32[]{:T(12...) while((s32[]{:T(128)}, f32[8,128,256]{2,1,0:T(8,128)S(1)}, ...), condition=%wide.region_27.30_spmd, body=%wide.region_24.29_spmd.sunk | while | flops 135268640 | bytes 12067359 | solution.py:40
  1562.8 3.3 scatter_fusion.5
  1573.5 3.4 scatter_fusion.5
  1595.1 3.3 scatter_fusion.5
  1627.3 3.4 scatter_fusion.5
  1659.5 3.3 scatter_fusion.5
  1670.8 91.0 %reduce-scatter.15.cloned.1.call-done = f32[128,256]{1,0:T(8,128)} async-done(((f32[1024,256]{1,0:T(8,128)}), f32[128,256]{1,0:T(8,128)}) %reduce-scatter.15.cloned.1.call-update) | async-done | bytes 131088 | tf_op jit(solution)/shard_map/reduce_scatter | solution.py:92
  1761.9 95.0 %reduce-scatter.17.cloned.1.call-done = f32[128,256]{1,0:T(8,128)} async-done(((f32[4096,256]{1,0:T(8,128)}), f32[128,256]{1,0:T(8,128)}) %reduce-scatter.17.cloned.1.call-update) | async-done | bytes 131088 | tf_op jit(solution)/shard_map/reduce_scatter | solution.py:98
  1860.7 252.9 %all-reduce.11.cloned.1.call-done = f32[256,256]{1,0:T(8,128)} async-done(((f32[256,256]{1,0:T(8,128)}), f32[256,256]{1,0:T(8,128)}) %all-reduce.11.cloned.1.call-update) | async-done | bytes 262160 | tf_op jit(solution)/shard_map/psum | solution.py:113
  (399 shorter events, 324.4 us)
Async XLA Ops:
  7.2 147.4 %copy-start.7 = (u32[256]{0:T(256)S(1)}, u32[256]{0:T(256)}, u32[]{:S(2)}) copy-start(u32[256]{0:T(256)} %constant.351) | copy-start | bytes 3076
  7.2 147.9 %copy-start.6 = (u32[256]{0:T(256)S(1)}, u32[256]{0:T(256)}, u32[]{:S(2)}) copy-start(u32[256]{0:T(256)} %constant.355) | copy-start | bytes 3076
  7.2 4.4 copy-start.5
  7.2 149.8 %copy-start.4 = (f32[128,256]{1,0:T(8,128)S(1)}, f32[128,256]{1,0:T(8,128)}, u32[]{:S(2)}) copy-start(f32[128,256]{1,0:T(8,128)} %param.16) | copy-start | bytes 393220
  7.2 201.8 %all-gather.4.cloned.1.call-start = ((), (), s32[]{:S(2)}) async-start(), calls=%async_computation.6 | async-start | bytes 2162688 | tf_op jit(solution)/shard_map/all_gather | solution.py:84
  157.8 255.4 %reduce-scatter.7.cloned.1.call-start = ((), (), s32[]{:S(2)}) async-start(), calls=%async_computation.7 | async-start | bytes 1179648 | tf_op jit(solution)/shard_map/reduce_scatter | solution.py:92
  319.1 1.0 copy-start.1
  320.1 188.2 %reduce-scatter.9.cloned.1.call-start = ((), (), s32[]{:S(2)}) async-start(), calls=%async_computation.8 | async-start | bytes 4325376 | tf_op jit(solution)/shard_map/reduce_scatter | solution.py:98
  320.8 444.2 %all-reduce.7.cloned.1.call-start = ((), (), s32[]{:S(2)}) async-start(), calls=%async_computation.9 | async-start | bytes 524288 | tf_op jit(solution)/shard_map/psum | solution.py:45
  510.6 368.6 %all-gather.6.cloned.1.call-start = ((), (), s32[]{:S(2)}) async-start(), calls=%async_computation.10 | async-start | bytes 2162688 | tf_op jit(solution)/shard_map/all_gather | solution.py:84
  828.8 258.3 %reduce-scatter.11.cloned.1.call-start = ((), (), s32[]{:S(2)}) async-start(), calls=%async_computation.11 | async-start | bytes 1179648 | tf_op jit(solution)/shard_map/reduce_scatter | solution.py:92
  993.4 1.0 copy-start.2
  994.4 188.8 %reduce-scatter.13.cloned.1.call-start = ((), (), s32[]{:S(2)}) async-start(), calls=%async_computation.12 | async-start | bytes 4325376 | tf_op jit(solution)/shard_map/reduce_scatter | solution.py:98
  995.1 444.0 %all-reduce.9.cloned.1.call-start = ((), (), s32[]{:S(2)}) async-start(), calls=%async_computation.13 | async-start | bytes 524288 | tf_op jit(solution)/shard_map/psum | solution.py:45
  1185.5 368.0 %all-gather.8.cloned.1.call-start = ((), (), s32[]{:S(2)}) async-start(), calls=%async_computation.14 | async-start | bytes 2162688 | tf_op jit(solution)/shard_map/all_gather | solution.py:84
  1503.1 258.8 %reduce-scatter.15.cloned.1.call-start = ((), (), s32[]{:S(2)}) async-start(), calls=%async_computation.15 | async-start | bytes 1179648 | tf_op jit(solution)/shard_map/reduce_scatter | solution.py:92
  1667.7 1.0 copy-start
  1667.7 1.8 copy-start.3
  1668.7 188.2 %reduce-scatter.17.cloned.1.call-start = ((), (), s32[]{:S(2)}) async-start(), calls=%async_computation.16 | async-start | bytes 4325376 | tf_op jit(solution)/shard_map/reduce_scatter | solution.py:98
  1669.4 444.2 %all-reduce.11.cloned.1.call-start = ((), (), s32[]{:S(2)}) async-start(), calls=%async_computation.17 | async-start | bytes 524288 | tf_op jit(solution)/shard_map/psum | solution.py:113
Sparse Core Ops, SparseCore 0:
  157.9 51.0 all-gather.3
  320.2 92.9 reduce-scatter.6
  417.1 91.1 reduce-scatter.8
  515.1 249.8 all-reduce.6
  828.9 50.2 all-gather.5
  994.5 92.5 reduce-scatter.10
  1091.5 91.6 reduce-scatter.12
  1189.2 249.8 all-reduce.8
  1503.2 50.2 all-gather.7
  1668.8 93.0 reduce-scatter.14
  1765.8 91.0 reduce-scatter.16
  1863.7 249.8 all-reduce.10
where the time goes:
time: 2140 us; the launch traced here: 2130 us
  waiting for transfers between devices  1410 us (66%)
  other arithmetic  287 us (13%)
  blocking collectives  204 us (10%)
  local copies, waits for them, and re-layouts  114 us (5%)
  matrix products  87.6 us (4%)
    psum x2, waiting for transfers between devices, orthonormal(): gram_sum = lax.psum(local_gram, ('row', 'col'))  505 us
    reduce_scatter x3, waiting for transfers between devices, apply_operator(): lax.psum_scatter(col_acc.reshape(row_devices * block_size, vec_width), 'r...  286 us
    reduce_scatter x3, waiting for transfers between devices, apply_operator(): lax.psum_scatter(row_acc.reshape(col_devices * block_size, vec_width), 'c...  275 us
    psum x1, waiting for transfers between devices, local(): ritz = lax.psum(local_ritz, ('row', 'col'))  253 us
    unnamed x2, blocking collectives  140 us
    scatter-add x30, other arithmetic, group_step(): col_part = col_part.at[col_ids].add(behind)  99.3 us
    all_gather x3, waiting for transfers between devices, apply_operator(): lax.all_gather(weighted, 'row', axis=0, tiled=True)  88.3 us
    another operation x13, other arithmetic, orthonormal(): factor = jnp.linalg.cholesky(gram_sum)  68.5 us
  transfers between devices with their start and end apart: 12, of which 12 were waited for; matrix products, arithmetic and copies ran while one was open for 0% of the time, Pallas kernels for 0%

commit v1 on v0

v1 whole, which is shorter than its diff:
```python
import functools
import math

import jax
import jax.numpy as jnp
from jax import lax
from jax.experimental import pallas as pl
from jax.experimental.pallas import tpu as pltpu
from jax.sharding import PartitionSpec as P

APPLIES = 3
MESH = pl.DeviceIdType.MESH
highest = lax.Precision.HIGHEST
f32 = jnp.float32
bf16 = jnp.bfloat16
BS = 128


def kernel(side, n_col, width, table, blocks, start, vec_out, gram_out,
           u, wt, wc, colp, corep, rsend, rrecv, rowp, zrecv, yv, ytv,
           dacc, dcore, dxy, dz, gr, ga, gb, gc, gd,
           s_core, r_core, s_xy, r_xy, s_z, r_z, s_fwd, r_fwd):
    chips = side * side
    n_row = 2 * chips
    row = lax.axis_index("row")
    z = lax.axis_index("col")
    core = lax.rem(row, 2)
    chip = row // 2
    y, x = chip // side, lax.rem(chip, side)
    other = 1 - core

    def sibling():
        return (chip * 2 + other, z)

    def xy_to(p):
        return lax.rem(y + p // side, side) * side + lax.rem(x + lax.rem(p, side), side)

    def xy_from(p):
        return lax.rem(y + side - p // side, side) * side + lax.rem(x + side - lax.rem(p, side), side)

    def z_to(p):
        return lax.rem(z + p, n_col)

    def z_from(p):
        return lax.rem(z + n_col - p, n_col)

    def xy_dev(t):
        return (t * 2 + core, z)

    def z_dev(t):
        return (row, t)

    def remote(src, dst, send, recv, dev):
        return pltpu.make_async_remote_copy(
            src_ref=src, dst_ref=dst, send_sem=send, recv_sem=recv,
            device_id=dev, device_id_type=MESH)

    def each(lo, hi, body):
        def step(i, c):
            body(i)
            return c
        lax.fori_loop(lo, hi, step, 0)

    barrier = pltpu.get_barrier_semaphore()
    pl.semaphore_signal(barrier, inc=1, device_id=sibling(), device_id_type=MESH)
    each(1, chips, lambda p: pl.semaphore_signal(
        barrier, inc=1, device_id=xy_dev(xy_to(p)), device_id_type=MESH))
    each(1, n_col, lambda p: pl.semaphore_signal(
        barrier, inc=1, device_id=z_dev(z_to(p)), device_id_type=MESH))

    dacc[...] = jnp.zeros_like(dacc)
    ones = jnp.ones((8, BS), f32)

    def fill_row(lr):
        def fill(pos, total):
            slot = table[lr * n_row + pos]
            live = (slot > 0).astype(f32)
            block = blocks[jnp.maximum(slot - 1, 0)].astype(f32) * live
            u[pl.ds(pl.multiple_of(lr * BS, BS), BS), pl.ds(pl.multiple_of(pos * BS, BS), BS)] = block.astype(bf16)
            size = jnp.abs(block)
            dacc[pos // chips, lax.rem(pos, chips)] += jnp.sum(size.reshape(BS // 8, 8, BS), axis=0)
            return total + size
        total = lax.fori_loop(0, n_row, fill, jnp.zeros((BS, BS), f32))
        rowp[0, lr, 0:8, 0:BS] = lax.dot_general(
            ones, total, (((1,), (1,)), ((), ())), precision=highest, preferred_element_type=f32)
    each(0, n_col, fill_row)

    pl.semaphore_wait(barrier, 1 + (chips - 1) + (n_col - 1))

    D = APPLIES

    def deg_z(p, lr, slot):
        return remote(rowp.at[0, lr, 0:8, 0:BS], dz.at[p], s_z.at[p], r_z.at[D, p], z_dev(slot))
    each(1, n_col, lambda p: deg_z(p, z_to(p), z_to(p)).start())
    deg_core = remote(dacc.at[other], dcore, s_core.at[0], r_core.at[D], sibling())
    deg_core.start()
    deg_core.wait()
    dacc[core] += dcore[...]

    def deg_xy(p):
        t = xy_to(p)
        return remote(dacc.at[core, t], dxy.at[p], s_xy.at[p], r_xy.at[D, p], xy_dev(t))
    each(1, chips, lambda p: deg_xy(p).start())
    dz[0] = rowp[0, z, 0:8, 0:BS]
    dxy[0] = dacc[core, chip]
    each(1, n_col, lambda p: deg_z(p, z_to(p), z_to(p)).wait())
    each(1, chips, lambda p: deg_xy(p).wait())
    degree = jnp.sum(dz[...], axis=0)[0:1] + jnp.sum(jnp.sum(dxy[...], axis=0), axis=0, keepdims=True)
    inv_row = 1.0 / jnp.sqrt(degree / BS + 1e-05)
    inv = jnp.broadcast_to(inv_row, (BS, BS)).T
    inv = inv[:, 0:1]
    yv[0] = start[...]

    def row_pos(k, t):
        return k * chips + t

    def apply_once(a):
        w = inv * yv[a]
        wc[lax.rem(a, 2), pl.ds(pl.multiple_of(row_pos(core, chip) * BS, BS), BS), :] = w.astype(bf16)
        wt[a, :, pl.ds(pl.multiple_of(z * BS, BS), BS)] = w.T.astype(bf16)
        even = lax.rem(a, 2)

        def wt_part(t):
            return wt.at[a, :, pl.ds(pl.multiple_of(t * BS, BS), BS)]

        def wc_part(k, t):
            return wc.at[even, pl.ds(pl.multiple_of(row_pos(k, t) * BS, BS), BS), :]

        def z_send(p):
            return remote(wt_part(z), wt_part(z), s_z.at[p], r_z.at[a, p], z_dev(z_to(p)))

        def z_arrive(p):
            t = z_from(p)
            return remote(wt_part(t), wt_part(t), s_z.at[p], r_z.at[a, p], z_dev(t))

        def xy_send(p):
            return remote(wc_part(core, chip), wc_part(core, chip), s_xy.at[p], r_xy.at[a, p], xy_dev(xy_to(p)))

        def xy_arrive(p):
            t = xy_from(p)
            return remote(wc_part(core, t), wc_part(core, t), s_xy.at[p], r_xy.at[a, p], xy_dev(t))

        def fwd_send(p):
            t = xy_from(p)
            return remote(wc_part(core, t), wc_part(core, t), s_fwd.at[p], r_fwd.at[a, p], sibling())

        def fwd_arrive(p):
            t = xy_from(p)
            return remote(wc_part(other, t), wc_part(other, t), s_fwd.at[p], r_fwd.at[a, p], sibling())

        each(1, n_col, lambda p: z_send(p).start())
        each(1, chips, lambda p: xy_send(p).start())
        fwd_send(0).start()
        each(1, n_col, lambda p: z_arrive(p).wait_recv())

        def col_half(k):
            def tile(n):
                first = (k * chips + 2 * n) * BS
                out = jnp.dot(wt[a], u[:, pl.ds(pl.multiple_of(first, 2 * BS), 2 * BS)], preferred_element_type=f32)
                colp[k, 2 * n] = out[:, :BS]
                colp[k, 2 * n + 1] = out[:, BS:]
            each(0, chips // 2, tile)

        core_swap = remote(colp.at[other], corep.at[a], s_core.at[0], r_core.at[a], sibling())
        col_half(other)
        core_swap.start()
        col_half(core)

        def pass_on(p):
            xy_arrive(p).wait_recv()
            fwd_send(p).start()
        each(1, chips, pass_on)
        core_swap.wait_recv()

        def rs_xy(p):
            return remote(rsend.at[p], rrecv.at[a, p], s_xy.at[p], r_xy.at[APPLIES + 1 + a, p], xy_dev(xy_to(p)))

        def combine(p):
            t = xy_to(p)
            xy_send(p).wait_send()
            rsend[p] = (colp[core, t] + corep[a, t]).astype(bf16)
            rs_xy(p).start()
        each(1, chips, combine)

        each(0, chips, lambda p: fwd_arrive(p).wait_recv())

        def row_tile(n):
            out = jnp.dot(u[pl.ds(pl.multiple_of(n * 2 * BS, 2 * BS), 2 * BS), :], wc[even], preferred_element_type=f32)
            rowp[0, 2 * n] = out[:BS]
            rowp[0, 2 * n + 1] = out[BS:]
        each(0, n_col // 2, row_tile)

        def rs_z(p):
            return remote(rowp.at[0, z_to(p)], zrecv.at[a, p], s_z.at[p], r_z.at[APPLIES + 1 + a, p], z_dev(z_to(p)))

        def row_go(p):
            z_send(p).wait_send()
            rs_z(p).start()
        each(1, n_col, row_go)

        def add_col(p, total):
            rs_xy(p).wait_recv()
            return total + rrecv[a, p].astype(f32)
        cols = lax.fori_loop(1, chips, add_col, colp[core, chip] + corep[a, chip])

        def add_row(p, total):
            rs_z(p).wait_recv()
            return total + zrecv[a, p]
        rows = lax.fori_loop(1, n_col, add_row, rowp[0, z])
        out = inv * (rows + cols.T)
        yv[a + 1] = out
        ytv[a] = out.T
        core_swap.wait_send()
        each(1, chips, lambda p: rs_xy(p).wait_send())
        each(1, n_col, lambda p: rs_z(p).wait_send())
        each(0, chips, lambda p: fwd_send(p).wait_send())

    each(0, APPLIES, apply_once)
    vec_out[0] = yv[2]
    vec_out[1] = yv[3]

    def local_gram(a, b, n):
        g = jnp.dot(ytv[a], yv[b], precision=highest, preferred_element_type=f32)
        g = g.reshape(2, chips, width // n_row, width)
        for k in range(2):
            for t in range(chips):
                gr[k, t, n] = g[k, t]
    local_gram(0, 1, 0)
    local_gram(1, 2, 1)
    local_gram(1, 3, 2)
    A = 2 * APPLIES + 1
    g_core = remote(gr.at[other], ga, s_core.at[0], r_core.at[APPLIES + 1], sibling())
    g_core.start()
    g_core.wait()
    gr[core] += ga[...]

    def g_xy(p):
        t = xy_to(p)
        return remote(gr.at[core, t], gb.at[p], s_xy.at[p], r_xy.at[A, p], xy_dev(t))
    each(1, chips, lambda p: g_xy(p).start())
    each(1, chips, lambda p: g_xy(p).wait())
    gb[0] = gr[core, chip]
    gc[0] = jnp.sum(gb[...], axis=0)

    def g_z(p):
        return remote(gc.at[0], gc.at[p], s_z.at[p], r_z.at[A, p], z_dev(z_to(p)))
    each(1, n_col, lambda p: g_z(p).start())
    each(1, n_col, lambda p: g_z(p).wait())

    def add_z(t, total):
        return total + gc[lax.rem(z + n_col - t, n_col)]
    gd[core, chip] = lax.fori_loop(1, n_col, add_z, gc[z])

    def g_back(p):
        t = xy_from(p)
        return remote(gd.at[core, t], gd.at[core, t], s_xy.at[p], r_xy.at[A + 1, p], xy_dev(t))

    def g_out(p):
        return remote(gd.at[core, chip], gd.at[core, chip], s_xy.at[p], r_xy.at[A + 1, p], xy_dev(xy_to(p)))
    each(1, chips, lambda p: g_out(p).start())
    each(1, chips, lambda p: g_back(p).wait_recv())
    each(1, chips, lambda p: g_out(p).wait_send())
    g_last = remote(gd.at[core], gd.at[core], s_core.at[0], r_core.at[APPLIES + 2], sibling())
    g_last.start()
    g_last.wait_send()
    remote(gd.at[other], gd.at[other], s_core.at[0], r_core.at[APPLIES + 2], sibling()).wait_recv()
    gram_out[...] = gd[...]


def fused(table, blocks, start, side, n_col, interpret=False):
    chips = side * side
    n_row = 2 * chips
    width = start.shape[1]
    sems = pltpu.SemaphoreType.DMA
    vmem = pltpu.VMEM
    part = width // n_row
    return pl.pallas_call(
        functools.partial(kernel, side, n_col, width),
        out_shape=(jax.ShapeDtypeStruct((2, BS, width), f32),
                   jax.ShapeDtypeStruct((2, chips, 3, part, width), f32)),
        in_specs=[pl.BlockSpec(memory_space=pltpu.SMEM)] + [pl.BlockSpec(memory_space=pltpu.VMEM)] * 2,
        out_specs=(pl.BlockSpec(memory_space=pltpu.VMEM), pl.BlockSpec(memory_space=pltpu.VMEM)),
        scratch_shapes=[
            vmem((n_col * BS, n_row * BS), bf16),
            vmem((APPLIES, width, n_col * BS), bf16),
            vmem((2, n_row * BS, width), bf16),
            vmem((2, chips, width, BS), f32),
            vmem((APPLIES, chips, width, BS), f32),
            vmem((chips, width, BS), bf16),
            vmem((APPLIES, chips, width, BS), bf16),
            vmem((1, n_col, BS, width), f32),
            vmem((APPLIES, n_col, BS, width), f32),
            vmem((APPLIES + 1, BS, width), f32),
            vmem((APPLIES, width, BS), f32),
            vmem((2, chips, 8, BS), f32),
            vmem((chips, 8, BS), f32),
            vmem((chips, 8, BS), f32),
            vmem((n_col, 8, BS), f32),
            vmem((2, chips, 3, part, width), f32),
            vmem((chips, 3, part, width), f32),
            vmem((chips, 3, part, width), f32),
            vmem((n_col, 3, part, width), f32),
            vmem((2, chips, 3, part, width), f32),
            sems((1,)), sems((APPLIES + 3,)),
            sems((chips,)), sems((2 * APPLIES + 3, chips)),
            sems((n_col,)), sems((2 * APPLIES + 2, n_col)),
            sems((chips,)), sems((APPLIES, chips)),
        ],
        compiler_params=pltpu.CompilerParams(
            collective_id=0, has_side_effects=True, vmem_limit_bytes=60 * 1024 * 1024),
        interpret=interpret,
    )(table, blocks, start)


def local(block_values, block_index, block_count, start_vectors, interpret=False):
    n_row = lax.axis_size("row")
    n_col = lax.axis_size("col")
    side = math.isqrt(n_row // 2)
    chips = side * side
    blocks = block_values[0, 0]
    slots = blocks.shape[0]
    width = start_vectors.shape[1]
    total_rows = BS * n_row * n_col
    first, second = block_index[0, 0, 0], block_index[0, 0, 1]
    owner = second // n_col
    place = (first % n_col) * n_row + (owner % 2) * chips + owner // 2
    slot_ids = jnp.arange(slots, dtype=jnp.int32)
    place = jnp.where(slot_ids < block_count[0, 0], place, -1)
    spots = jnp.arange(n_row * n_col, dtype=jnp.int32)
    table = jnp.sum(jnp.where(place[None, :] == spots[:, None], slot_ids[None, :] + 1, 0), axis=1)

    vecs, grams = fused(table, blocks, start_vectors, side, n_col, interpret)
    second_vec, third_vec = vecs[0], vecs[1]
    grams = grams.transpose(2, 0, 1, 3, 4).reshape(3, width, width)
    factors = jnp.linalg.cholesky(grams[:2])
    inverses = jax.scipy.linalg.solve_triangular(
        factors, jnp.broadcast_to(jnp.eye(width, dtype=f32), (2, width, width)), lower=True)
    mul = functools.partial(jnp.matmul, precision=highest)
    gram = mul(mul(inverses[0], grams[1]), inverses[0].T)
    ritz = mul(mul(inverses[1], grams[2]), inverses[1].T)
    subspace = mul(second_vec, inverses[1].T)
    mapped = mul(third_vec, inverses[1].T)
    gram_scaled = gram / jnp.sqrt(jnp.mean(gram * gram) + 1e-06)
    spread = jnp.sqrt(jnp.mean(ritz * ritz) + 1e-06)
    residual = (mapped - mul(subspace, ritz)) * (math.sqrt(total_rows / width) / spread)
    return (subspace * math.sqrt(total_rows), ritz / spread, residual, gram_scaled)


def solution(mesh):
    return jax.shard_map(
        local,
        mesh=mesh,
        in_specs=(
            P("row", "col", None, None, None),
            P("row", "col", None, None),
            P("row", "col"),
            P(("row", "col"), None),
        ),
        out_specs=(P(("row", "col"), None), P(), P(("row", "col"), None), P()),
        check_vma=False,
    )
```

time: 2140 us -> 332 us (0.16)
  waiting for transfers between devices: 1410 us -> 0 us
  Pallas kernels: 0 us -> 207 us
  blocking collectives: 204 us -> 0 us
  other arithmetic: 287 us -> 110 us
  local copies, waits for them, and re-layouts: 114 us -> 5.48 us
  matrix products: 87.6 us -> 7.04 us
    psum x3 -> x0, waiting for transfers between devices: 758 us -> none  [the longest x2 505 us: orthonormal(): gram_sum = lax.psum(local_gram, ('row', 'col'))]
    reduce_scatter x6 -> x0, waiting for transfers between devices: 562 us -> none  [the longest x3 286 us: apply_operator(): lax.psum_scatter(col_acc.reshape(row_devices * block_size, vec_width), 'r...]
    pallas_call x0 -> x1, Pallas kernels: none -> 207 us  [fused(): pl.pallas_call(functools.partial(kernel, side, n_col, width), out_shape=(...]
    scatter-add x62 -> x0, other arithmetic: 142 us -> none  [the longest x30 99.3 us: group_step(): col_part = col_part.at[col_ids].add(behind)]
    unnamed x2 -> x0, blocking collectives: 140 us -> none
    all_gather x3 -> x0, waiting for transfers between devices: 88.3 us -> none  [apply_operator(): lax.all_gather(weighted, 'row', axis=0, tiled=True)]
    gather x60 -> x0, local copies, waits for them, and re-layouts: 82.5 us -> none  [the longest x30 65.1 us: group_step(): col_slab[col_ids]]
    dot_general x64 -> x7, matrix products: 84.9 us -> 5.18 us  [the longest x2 1.39 us: local(): ritz = mul(mul(inverses[1], grams[2]), inverses[1].T)]
  transfers between devices with their start and end apart: 12 -> 0, of which waited for: 12 -> 0; matrix products, arithmetic and copies ran while one was open for 0% -> 0% of each run, Pallas kernels for 0% -> 0%
where the time goes in v1:
time: 332 us
  Pallas kernels  207 us (62%)
  other arithmetic  110 us (33%)
  matrix products  7.04 us (2%)
  local copies, waits for them, and re-layouts  5.48 us (2%)
    pallas_call x1, Pallas kernels, fused(): pl.pallas_call(functools.partial(kernel, side, n_col, width), out_shape=(...  207 us
    another operation x10, other arithmetic, local(): factors = jnp.linalg.cholesky(grams[:2])  67.1 us
    another operation x4, other arithmetic, local(): jax.scipy.linalg.solve_triangular(factors, jnp.broadcast_to(jnp.eye(width...  39.5 us

profile of v1, /device:TPU:1, one launch (start us, length us, event | category | flops | bytes accessed | tf_op | source)
XLA Modules:
  0.0 332.0 jit_solution(7937122832764013020)
XLA Ops:
  1.3 0.8 compare_select_fusion.2
  2.1 0.7 select_reduce_fusion.2.table
  2.7 206.8 %shard_map.75 = (f32[2,128,256]{2,1,0:T(8,128)}, f32[2,16,3,8,256]{4,3,2,1,0:T(8,128)}) custom-call(s32[256]{0:T(256)} %select_reduce_fusion.2.table, bf16[128,128,128]{2,1,0:T(8,128)(2,1)} %bitcast.85, f32[128,256]{1,0:T(8,128)} %start.1), custom_call_target="tpu_custom_call" | custom-call | tf_op jit(solution)/shard_map/pallas_call | solution.py:277
  209.6 1.1 slice.108
  210.7 0.2 copy.23
  210.9 0.1 fusion.1
  211.0 0.0 copy-start
  211.0 23.5 %custom-call.17 = f32[2,128,128]{2,1,0:T(8,128)S(1)} custom-call(f32[2,128,128]{2,1,0:T(8,128)S(1)} %cholesky.122), custom_call_target="Cholesky" | custom-call | tf_op jit(solution)/shard_map/jit(cholesky)/cholesky | solution.py:335
  234.6 19.7 %custom-call.18 = f32[2,1,128,128]{2,3,1,0:T(8,128)S(1)} custom-call(f32[2,1,128,128]{3,2,1,0:T(8,128)S(1)} %select_bitcast_fusion), custom_call_target="InvertDiagBlocksLowerTriangular" | custom-call | tf_op jit(solution)/shard_map/jit(cholesky)/cholesky | solution.py:335
  254.2 0.3 constant_dynamic-update-slice_fusion.1
  254.5 0.4 convolution_subtract_fusion.2
  254.9 23.6 %custom-call.19 = f32[2,128,128]{2,1,0:T(8,128)S(1)} custom-call(f32[2,128,128]{2,1,0:T(8,128)S(1)} %convolution_subtract_fusion.2), custom_call_target="Cholesky" | custom-call | tf_op jit(solution)/shard_map/jit(cholesky)/cholesky | solution.py:335
  278.6 0.1 compare_reduce_fusion
  278.7 0.1 compare_reduce_fusion.1
  278.9 0.1 select_select_fusion
  279.0 0.1 triangular_solve.66
  279.1 4.0 %while.1 = (s32[]{:T(128)}, f32[2,256,256]{2,1,0:T(8,128)S(1)}, s32[2,2]{1,0:T(2,128)S(1)}, f32[2,2,128,128]{3,2,0,1:T(8,128)S(1)}, s32[]{:T(128)}) while((s32[]{:T(128)}, f32[2,256,256]{2,1,0:T(8,128)S(1)}, s32[2,2]{1,0:T(2,128)S(1)}, f32[2,2,128,128]{3,2,0,1:T(8,128)S(1)}, s32[]{:T(128)}) %tuple.32), condition=%wide.while_cond, body=%wide.while_body.sunk | while | flops 2 | bytes 262253 | solution.py:336
  279.1 0.6 fusion.49
  279.7 1.4 bitcast_dynamic-update-slice_fusion.2
  281.1 0.6 fusion.49
  281.7 1.4 bitcast_dynamic-update-slice_fusion.2
  283.1 39.3 %custom-call.20 = f32[2,2,128,128]{2,3,1,0:T(8,128)S(1)} custom-call(f32[2,2,128,128]{3,2,1,0:T(8,128)S(1)} %bitcast.90), custom_call_target="InvertDiagBlocksLowerTriangular" | custom-call | tf_op jit(solution)/shard_map/jit(_solve_triangular)/vmap()/triangular_solve | solution.py:336
  322.5 0.0 copy-start.1
  322.5 0.4 fusion.8
  323.0 0.4 convolution_subtract_fusion
  323.3 0.4 fusion.7
  323.8 0.0 copy-done
  323.8 0.4 fusion.21
  324.2 1.0 multiply_reduce_fusion
  325.9 0.7 broadcast_divide_fusion
  326.7 0.4 fusion.33
  327.1 1.0 multiply_reduce_fusion.1
  328.8 0.0 copy-done.1
  328.8 0.4 fusion.11
  329.2 1.1 broadcast_multiply_fusion
  330.3 0.9 fusion
  331.2 0.7 broadcast_divide_fusion.1
  (17 shorter events, 0.3 us)
Async XLA Ops:
  211.0 112.8 %copy-start = (f32[2,16,3,8,256]{4,3,2,1,0:T(8,128)S(1)}, f32[2,16,3,8,256]{4,3,2,1,0:T(8,128)}, u32[]{:S(2)}) copy-start(f32[2,16,3,8,256]{4,3,2,1,0:T(8,128)} %get-tuple-element.7) | copy-start | bytes 2359300
  322.5 6.3 %copy-start.1 = (f32[2,128,256]{2,1,0:T(8,128)S(1)}, f32[2,128,256]{2,1,0:T(8,128)}, u32[]{:S(2)}) copy-start(f32[2,128,256]{2,1,0:T(8,128)} %get-tuple-element.6) | copy-start | bytes 786436

commit v2 on v1

--- a/solution.py
+++ b/solution.py
@@ -312,6 +312,94 @@
     )(table, blocks, start)
 
 
+def tri_inverses(n, s, e):
+    sub = lax.broadcasted_iota(jnp.int32, (8, BS), 0)
+    lane = lax.broadcasted_iota(jnp.int32, (8, BS), 1)
+    eye = (lax.broadcasted_iota(jnp.int32, (BS, BS), 0) == lax.broadcasted_iota(jnp.int32, (BS, BS), 1)).astype(f32)
+    for m in range(n):
+        e[m] = eye
+
+    def panel(k, c):
+        first = pl.multiple_of(k * 8, 8)
+        for m in range(n):
+            r = s[m, pl.ds(first, 8), :]
+            g = e[m, pl.ds(first, 8), :]
+            own = jnp.where(lane >= first, jnp.where(lane < first + 8, r, 0.0), 0.0)
+            cols = []
+            for j in range(8):
+                at_j = jnp.where(lane == first + j, own, 0.0)
+                cols.append(jnp.broadcast_to(jnp.sum(at_j, axis=1, keepdims=True), (8, BS)))
+            scale = jnp.zeros((8, BS), f32)
+            for j in range(8):
+                pivot = jnp.broadcast_to(cols[j][j:j + 1], (8, BS))
+                mult = jnp.where(sub > j, cols[j] / pivot, 0.0)
+                scale = jnp.where(sub == j, pivot, scale)
+                r = r - mult * r[j:j + 1]
+                g = g - mult * g[j:j + 1]
+                for i in range(j + 1, 8):
+                    cols[i] = cols[i] - mult * cols[i][j:j + 1]
+            scale = 1.0 / jnp.sqrt(scale)
+            v = r * scale
+            g = g * scale
+            e[m, pl.ds(first, 8), :] = g
+            below = jnp.where(lane >= first + 8, v, 0.0)
+            step = lax.dot_general(below, jnp.concatenate([v, g], axis=1), (((0,), (0,)), ((), ())),
+                                   precision=highest, preferred_element_type=f32)
+            s[m] -= step[:, :BS]
+            e[m] -= step[:, BS:]
+        return c
+    lax.fori_loop(0, BS // 8, panel, 0)
+
+
+def finish_kernel(total_rows, vecs, grams, basis, projected, residual, scaled, s, e, li):
+    width = vecs.shape[2]
+    mul = functools.partial(jnp.dot, precision=highest, preferred_element_type=f32)
+    g = [grams[:, :, m].reshape(width, width) for m in range(3)]
+    half = []
+    for m in range(2):
+        s[m] = g[m][:BS, :BS]
+    tri_inverses(2, s, e)
+    for m in range(2):
+        li[m, :BS, :BS] = e[m]
+        li[m, :BS, BS:] = jnp.zeros((BS, BS), f32)
+        half.append(mul(e[m], g[m][:BS, BS:]))
+        s[m] = g[m][BS:, BS:] - lax.dot_general(
+            half[m], half[m], (((0,), (0,)), ((), ())), precision=highest, preferred_element_type=f32)
+    tri_inverses(2, s, e)
+    for m in range(2):
+        li[m, BS:, BS:] = e[m]
+        cross = lax.dot_general(half[m], li[m, :BS, :BS], (((0,), (0,)), ((), ())),
+                                precision=highest, preferred_element_type=f32)
+        li[m, BS:, :BS] = -mul(e[m], cross)
+    gram = mul(mul(li[0], g[1]), li[0].T)
+    right = li[1].T
+    ritz = mul(mul(li[1], g[2]), right)
+    subspace = mul(vecs[0], right)
+    mapped = mul(vecs[1], right)
+    area = width * width
+    scaled[...] = gram / jnp.sqrt(jnp.sum(gram * gram, keepdims=True) / area + 1e-06)
+    spread = jnp.sqrt(jnp.sum(ritz * ritz, keepdims=True) / area + 1e-06)
+    projected[...] = ritz / spread
+    basis[...] = subspace * math.sqrt(total_rows)
+    residual[...] = (mapped - mul(subspace, ritz)) * (math.sqrt(total_rows / width) / spread)
+
+
+def finish(vecs, grams, total_rows, interpret=False):
+    width = vecs.shape[2]
+    tall = jax.ShapeDtypeStruct((BS, width), f32)
+    square = jax.ShapeDtypeStruct((width, width), f32)
+    return pl.pallas_call(
+        functools.partial(finish_kernel, total_rows),
+        out_shape=(tall, square, tall, square),
+        in_specs=[pl.BlockSpec(memory_space=pltpu.VMEM)] * 2,
+        out_specs=tuple([pl.BlockSpec(memory_space=pltpu.VMEM)] * 4),
+        scratch_shapes=[pltpu.VMEM((2, BS, BS), f32), pltpu.VMEM((2, BS, BS), f32),
+                        pltpu.VMEM((2, width, width), f32)],
+        compiler_params=pltpu.CompilerParams(vmem_limit_bytes=32 * 1024 * 1024),
+        interpret=interpret,
+    )(vecs, grams)
+
+
 def local(block_values, block_index, block_count, start_vectors, interpret=False):
     n_row = lax.axis_size("row")
     n_col = lax.axis_size("col")
@@ -330,20 +418,7 @@
     table = jnp.sum(jnp.where(place[None, :] == spots[:, None], slot_ids[None, :] + 1, 0), axis=1)
 
     vecs, grams = fused(table, blocks, start_vectors, side, n_col, interpret)
-    second_vec, third_vec = vecs[0], vecs[1]
-    grams = grams.transpose(2, 0, 1, 3, 4).reshape(3, width, width)
-    factors = jnp.linalg.cholesky(grams[:2])
-    inverses = jax.scipy.linalg.solve_triangular(
-        factors, jnp.broadcast_to(jnp.eye(width, dtype=f32), (2, width, width)), lower=True)
-    mul = functools.partial(jnp.matmul, precision=highest)
-    gram = mul(mul(inverses[0], grams[1]), inverses[0].T)
-    ritz = mul(mul(inverses[1], grams[2]), inverses[1].T)
-    subspace = mul(second_vec, inverses[1].T)
-    mapped = mul(third_vec, inverses[1].T)
-    gram_scaled = gram / jnp.sqrt(jnp.mean(gram * gram) + 1e-06)
-    spread = jnp.sqrt(jnp.mean(ritz * ritz) + 1e-06)
-    residual = (mapped - mul(subspace, ritz)) * (math.sqrt(total_rows / width) / spread)
-    return (subspace * math.sqrt(total_rows), ritz / spread, residual, gram_scaled)
+    return finish(vecs, grams, total_rows, interpret)
 
 
 def solution(mesh):

time: 332 us -> 251 us (0.76)
  other arithmetic: 110 us -> 1.46 us
  Pallas kernels: 207 us -> 246 us
  matrix products: 7.04 us -> 0 us
  local copies, waits for them, and re-layouts: 5.48 us -> 2.08 us
    another operation x14 -> x0, other arithmetic: 107 us -> none  [the longest x10 67.1 us: local(): factors = jnp.linalg.cholesky(grams[:2])]
    pallas_call x0 -> x1, Pallas kernels: none -> 39.3 us  [finish(): pl.pallas_call(functools.partial(finish_kernel, total_rows), out_shape=(t...]
    dot_general x7 -> x0, matrix products: 5.18 us -> none  [the longest x2 1.39 us: local(): ritz = mul(mul(inverses[1], grams[2]), inverses[1].T)]
    another operation x10 -> x0, local copies, waits for them, and re-layouts: 4.12 us -> none
where the time goes in v2:
time: 251 us
  Pallas kernels  246 us (98%)
    pallas_call x1, Pallas kernels, fused(): pl.pallas_call(functools.partial(kernel, side, n_col, width), out_shape=(...  207 us
    pallas_call x1, Pallas kernels, finish(): pl.pallas_call(functools.partial(finish_kernel, total_rows), out_shape=(t...  39.3 us

profile of v2, /device:TPU:1, one launch (start us, length us, event | category | flops | bytes accessed | tf_op | source)
XLA Modules:
  0.0 250.8 jit_solution(7502265818950996042)
XLA Ops:
  1.3 0.8 compare_select_fusion.2
  2.1 0.7 select_reduce_fusion.table
  2.7 206.7 %shard_map.75 = (f32[2,128,256]{2,1,0:T(8,128)}, f32[2,16,3,8,256]{4,3,2,1,0:T(8,128)}) custom-call(s32[256]{0:T(256)} %select_reduce_fusion.table, bf16[128,128,128]{2,1,0:T(8,128)(2,1)} %bitcast.17, f32[128,256]{1,0:T(8,128)} %start.1), custom_call_target="tpu_custom_call" | custom-call | tf_op jit(solution)/shard_map/pallas_call | solution.py:277
  209.4 0.0 copy-start
  209.4 1.1 copy-done
  210.6 0.0 copy-start.1
  210.6 0.9 copy-done.1
  211.5 39.3 %shard_map.76 = (f32[128,256]{1,0:T(8,128)}, f32[256,256]{1,0:T(8,128)}, f32[128,256]{1,0:T(8,128)}, f32[256,256]{1,0:T(8,128)}) custom-call(f32[2,128,256]{2,1,0:T(8,128)S(1)} %copy-done.1, f32[2,16,3,8,256]{4,3,2,1,0:T(8,128)S(1)} %copy-done), custom_call_target="tpu_custom_call" | custom-call | tf_op jit(solution)/shard_map/pallas_call | solution.py:391
Async XLA Ops:
  209.4 1.1 copy-start
  210.6 0.9 copy-start.1

commit v3 on v1

--- a/solution.py
+++ b/solution.py
@@ -16,10 +16,11 @@
 BS = 128
 
 
-def kernel(side, n_col, width, table, blocks, start, vec_out, gram_out,
-           u, wt, wc, colp, corep, rsend, rrecv, rowp, zrecv, yv, ytv,
-           dacc, dcore, dxy, dz, gr, ga, gb, gc, gd,
-           s_core, r_core, s_xy, r_xy, s_z, r_z, s_fwd, r_fwd):
+def kernel(side, n_col, width, table, blocks, start, basis, projected, residual, scaled,
+           u, wt, wc, colp, colq, corep, rsend, rrecv, rowp, zsend, zrecv, yv, ytv,
+           dacc, dcore, dxy, dz, gram_bufs, ritz_bufs, chol,
+           s_core, r_core, s_xy, r_xy, s_z, r_z, s_fwd, r_fwd,
+           t_core, q_core, t_xy, q_xy, t_z, q_z):
     chips = side * side
     n_row = 2 * chips
     row = lax.axis_index("row")
@@ -114,11 +115,11 @@
     def row_pos(k, t):
         return k * chips + t
 
-    def apply_once(a):
+    def apply_once(a, idle_gather=None, idle_scatter=None):
         w = inv * yv[a]
-        wc[lax.rem(a, 2), pl.ds(pl.multiple_of(row_pos(core, chip) * BS, BS), BS), :] = w.astype(bf16)
+        wc[(a % 2), pl.ds(pl.multiple_of(row_pos(core, chip) * BS, BS), BS), :] = w.astype(bf16)
         wt[a, :, pl.ds(pl.multiple_of(z * BS, BS), BS)] = w.T.astype(bf16)
-        even = lax.rem(a, 2)
+        even = (a % 2)
 
         def wt_part(t):
             return wt.at[a, :, pl.ds(pl.multiple_of(t * BS, BS), BS)]
@@ -151,20 +152,22 @@
         each(1, n_col, lambda p: z_send(p).start())
         each(1, chips, lambda p: xy_send(p).start())
         fwd_send(0).start()
+        if idle_gather is not None:
+            idle_gather()
         each(1, n_col, lambda p: z_arrive(p).wait_recv())
 
-        def col_half(k):
+        def col_half(k, out_ref):
             def tile(n):
                 first = (k * chips + 2 * n) * BS
                 out = jnp.dot(wt[a], u[:, pl.ds(pl.multiple_of(first, 2 * BS), 2 * BS)], preferred_element_type=f32)
-                colp[k, 2 * n] = out[:, :BS]
-                colp[k, 2 * n + 1] = out[:, BS:]
+                out_ref[2 * n] = out[:, :BS].astype(out_ref.dtype)
+                out_ref[2 * n + 1] = out[:, BS:].astype(out_ref.dtype)
             each(0, chips // 2, tile)
 
-        core_swap = remote(colp.at[other], corep.at[a], s_core.at[0], r_core.at[a], sibling())
-        col_half(other)
+        core_swap = remote(colq, corep.at[a], s_core.at[0], r_core.at[a], sibling())
+        col_half(other, colq)
         core_swap.start()
-        col_half(core)
+        col_half(core, colp)
 
         def pass_on(p):
             xy_arrive(p).wait_recv()
@@ -178,7 +181,7 @@
         def combine(p):
             t = xy_to(p)
             xy_send(p).wait_send()
-            rsend[p] = (colp[core, t] + corep[a, t]).astype(bf16)
+            rsend[p] = (colp[t] + corep[a, t].astype(f32)).astype(bf16)
             rs_xy(p).start()
         each(1, chips, combine)
 
@@ -191,21 +194,24 @@
         each(0, n_col // 2, row_tile)
 
         def rs_z(p):
-            return remote(rowp.at[0, z_to(p)], zrecv.at[a, p], s_z.at[p], r_z.at[APPLIES + 1 + a, p], z_dev(z_to(p)))
+            return remote(zsend.at[p], zrecv.at[a, p], s_z.at[p], r_z.at[APPLIES + 1 + a, p], z_dev(z_to(p)))
 
         def row_go(p):
             z_send(p).wait_send()
+            zsend[p] = rowp[0, z_to(p)].astype(bf16)
             rs_z(p).start()
         each(1, n_col, row_go)
+        if idle_scatter is not None:
+            idle_scatter()
 
         def add_col(p, total):
             rs_xy(p).wait_recv()
             return total + rrecv[a, p].astype(f32)
-        cols = lax.fori_loop(1, chips, add_col, colp[core, chip] + corep[a, chip])
+        cols = lax.fori_loop(1, chips, add_col, colp[chip] + corep[a, chip].astype(f32))
 
         def add_row(p, total):
             rs_z(p).wait_recv()
-            return total + zrecv[a, p]
+            return total + zrecv[a, p].astype(f32)
         rows = lax.fori_loop(1, n_col, add_row, rowp[0, z])
         out = inv * (rows + cols.T)
         yv[a + 1] = out
@@ -215,56 +221,110 @@
         each(1, n_col, lambda p: rs_z(p).wait_send())
         each(0, chips, lambda p: fwd_send(p).wait_send())
 
-    each(0, APPLIES, apply_once)
-    vec_out[0] = yv[2]
-    vec_out[1] = yv[3]
-
-    def local_gram(a, b, n):
+    def local_gram(a, b, into, n):
         g = jnp.dot(ytv[a], yv[b], precision=highest, preferred_element_type=f32)
         g = g.reshape(2, chips, width // n_row, width)
         for k in range(2):
             for t in range(chips):
-                gr[k, t, n] = g[k, t]
-    local_gram(0, 1, 0)
-    local_gram(1, 2, 1)
-    local_gram(1, 3, 2)
-    A = 2 * APPLIES + 1
-    g_core = remote(gr.at[other], ga, s_core.at[0], r_core.at[APPLIES + 1], sibling())
-    g_core.start()
-    g_core.wait()
-    gr[core] += ga[...]
-
-    def g_xy(p):
-        t = xy_to(p)
-        return remote(gr.at[core, t], gb.at[p], s_xy.at[p], r_xy.at[A, p], xy_dev(t))
-    each(1, chips, lambda p: g_xy(p).start())
-    each(1, chips, lambda p: g_xy(p).wait())
-    gb[0] = gr[core, chip]
-    gc[0] = jnp.sum(gb[...], axis=0)
-
-    def g_z(p):
-        return remote(gc.at[0], gc.at[p], s_z.at[p], r_z.at[A, p], z_dev(z_to(p)))
-    each(1, n_col, lambda p: g_z(p).start())
-    each(1, n_col, lambda p: g_z(p).wait())
-
-    def add_z(t, total):
-        return total + gc[lax.rem(z + n_col - t, n_col)]
-    gd[core, chip] = lax.fori_loop(1, n_col, add_z, gc[z])
-
-    def g_back(p):
-        t = xy_from(p)
-        return remote(gd.at[core, t], gd.at[core, t], s_xy.at[p], r_xy.at[A + 1, p], xy_dev(t))
-
-    def g_out(p):
-        return remote(gd.at[core, chip], gd.at[core, chip], s_xy.at[p], r_xy.at[A + 1, p], xy_dev(xy_to(p)))
-    each(1, chips, lambda p: g_out(p).start())
-    each(1, chips, lambda p: g_back(p).wait_recv())
-    each(1, chips, lambda p: g_out(p).wait_send())
-    g_last = remote(gd.at[core], gd.at[core], s_core.at[0], r_core.at[APPLIES + 2], sibling())
-    g_last.start()
-    g_last.wait_send()
-    remote(gd.at[other], gd.at[other], s_core.at[0], r_core.at[APPLIES + 2], sibling()).wait_recv()
-    gram_out[...] = gd[...]
+                into[k, t, n] = g[k, t]
+
+    def sum_all(bufs, base, idle):
+        gr, ga, gb, gc, gd = bufs
+        q = 2 * base
+        g_core = remote(gr.at[other], ga, t_core.at[0], q_core.at[q], sibling())
+        g_core.start()
+        idle(0)
+        g_core.wait()
+        gr[core] += ga[...]
+
+        def g_xy(p):
+            t = xy_to(p)
+            return remote(gr.at[core, t], gb.at[p], t_xy.at[p], q_xy.at[q, p], xy_dev(t))
+        each(1, chips, lambda p: g_xy(p).start())
+        idle(1)
+        each(1, chips, lambda p: g_xy(p).wait())
+        gb[0] = gr[core, chip]
+        gc[0] = jnp.sum(gb[...], axis=0)
+
+        def g_z(p):
+            return remote(gc.at[0], gc.at[p], t_z.at[p], q_z.at[base, p], z_dev(z_to(p)))
+        each(1, n_col, lambda p: g_z(p).start())
+        idle(2)
+        each(1, n_col, lambda p: g_z(p).wait())
+
+        def add_z(t, total):
+            return total + gc[lax.rem(z + n_col - t, n_col)]
+        gd[core, chip] = lax.fori_loop(1, n_col, add_z, gc[z])
+
+        def g_back(p):
+            t = xy_from(p)
+            return remote(gd.at[core, t], gd.at[core, t], t_xy.at[p], q_xy.at[q + 1, p], xy_dev(t))
+
+        def g_out(p):
+            return remote(gd.at[core, chip], gd.at[core, chip], t_xy.at[p], q_xy.at[q + 1, p], xy_dev(xy_to(p)))
+        each(1, chips, lambda p: g_out(p).start())
+        idle(3)
+        each(1, chips, lambda p: g_back(p).wait_recv())
+        each(1, chips, lambda p: g_out(p).wait_send())
+        g_last = remote(gd.at[core], gd.at[core], t_core.at[0], q_core.at[q + 1], sibling())
+        g_last.start()
+        idle(4)
+        g_last.wait_send()
+        remote(gd.at[other], gd.at[other], t_core.at[0], q_core.at[q + 1], sibling()).wait_recv()
+
+    mul = functools.partial(jnp.dot, precision=highest, preferred_element_type=f32)
+    tmul = lambda a, b: lax.dot_general(a, b, (((0,), (0,)), ((), ())), precision=highest, preferred_element_type=f32)
+    s, e, li, half, full = chol
+
+    def sum_grams():
+        local_gram(0, 1, gram_bufs[0], 0)
+        local_gram(1, 2, gram_bufs[0], 1)
+        sum_all(gram_bufs, 0, lambda i: None)
+
+    def first_factors():
+        for m in range(2):
+            full[m] = gram_bufs[4][:, :, m].reshape(width, width)
+            s[m] = full[m, :BS, :BS]
+        unit(e)
+        panels(s, e, 0, BS // 8)
+        for m in range(2):
+            li[m, :BS, :BS] = e[m]
+            li[m, :BS, BS:] = jnp.zeros((BS, BS), f32)
+            half[m] = mul(e[m], full[m, :BS, BS:])
+            s[m] = full[m, BS:, BS:] - tmul(half[m], half[m])
+        unit(e)
+
+    each(0, APPLIES - 1, apply_once)
+    apply_once(APPLIES - 1, sum_grams, first_factors)
+    local_gram(1, 3, ritz_bufs[0], 0)
+    cuts = (0, 2, 7, 11, 16)
+
+    def second_factors(i):
+        if i < 4:
+            panels(s, e, cuts[i], cuts[i + 1])
+        else:
+            for m in range(2):
+                li[m, BS:, BS:] = e[m]
+                li[m, BS:, :BS] = -mul(e[m], tmul(half[m], li[m, :BS, :BS]))
+            gram = mul(mul(li[0], full[1]), li[0].T)
+            scaled[...] = gram / jnp.sqrt(jnp.sum(gram * gram, keepdims=True) / (width * width) + 1e-06)
+            full[0] = li[1].T
+            yv[0] = mul(yv[2], full[0])
+            yv[1] = mul(yv[3], full[0])
+
+    sum_all(ritz_bufs, 1, second_factors)
+    total_rows = BS * n_row * n_col
+    ritz = mul(mul(li[1], ritz_bufs[4][:, :, 0].reshape(width, width)), full[0])
+    spread = jnp.sqrt(jnp.sum(ritz * ritz, keepdims=True) / (width * width) + 1e-06)
+    projected[...] = ritz / spread
+    basis[...] = yv[0] * math.sqrt(total_rows)
+    residual[...] = (yv[1] - mul(yv[0], ritz)) * (math.sqrt(total_rows / width) / spread)
+
+
+def unit(e):
+    eye = (lax.broadcasted_iota(jnp.int32, (BS, BS), 0) == lax.broadcasted_iota(jnp.int32, (BS, BS), 1)).astype(f32)
+    for m in range(2):
+        e[m] = eye
 
 
 def fused(table, blocks, start, side, n_col, interpret=False):
@@ -274,42 +334,87 @@
     sems = pltpu.SemaphoreType.DMA
     vmem = pltpu.VMEM
     part = width // n_row
+    tall = jax.ShapeDtypeStruct((BS, width), f32)
+    square = jax.ShapeDtypeStruct((width, width), f32)
+
+    def sum_bufs(n):
+        return (vmem((2, chips, n, part, width), f32), vmem((chips, n, part, width), f32),
+                vmem((chips, n, part, width), f32), vmem((n_col, n, part, width), f32),
+                vmem((2, chips, n, part, width), f32))
     return pl.pallas_call(
         functools.partial(kernel, side, n_col, width),
-        out_shape=(jax.ShapeDtypeStruct((2, BS, width), f32),
-                   jax.ShapeDtypeStruct((2, chips, 3, part, width), f32)),
+        out_shape=(tall, square, tall, square),
         in_specs=[pl.BlockSpec(memory_space=pltpu.SMEM)] + [pl.BlockSpec(memory_space=pltpu.VMEM)] * 2,
-        out_specs=(pl.BlockSpec(memory_space=pltpu.VMEM), pl.BlockSpec(memory_space=pltpu.VMEM)),
+        out_specs=tuple([pl.BlockSpec(memory_space=pltpu.VMEM)] * 4),
         scratch_shapes=[
             vmem((n_col * BS, n_row * BS), bf16),
             vmem((APPLIES, width, n_col * BS), bf16),
             vmem((2, n_row * BS, width), bf16),
-            vmem((2, chips, width, BS), f32),
-            vmem((APPLIES, chips, width, BS), f32),
+            vmem((chips, width, BS), f32),
+            vmem((chips, width, BS), bf16),
+            vmem((APPLIES, chips, width, BS), bf16),
             vmem((chips, width, BS), bf16),
             vmem((APPLIES, chips, width, BS), bf16),
             vmem((1, n_col, BS, width), f32),
-            vmem((APPLIES, n_col, BS, width), f32),
+            vmem((n_col, BS, width), bf16),
+            vmem((APPLIES, n_col, BS, width), bf16),
             vmem((APPLIES + 1, BS, width), f32),
             vmem((APPLIES, width, BS), f32),
             vmem((2, chips, 8, BS), f32),
             vmem((chips, 8, BS), f32),
             vmem((chips, 8, BS), f32),
             vmem((n_col, 8, BS), f32),
-            vmem((2, chips, 3, part, width), f32),
-            vmem((chips, 3, part, width), f32),
-            vmem((chips, 3, part, width), f32),
-            vmem((n_col, 3, part, width), f32),
-            vmem((2, chips, 3, part, width), f32),
-            sems((1,)), sems((APPLIES + 3,)),
-            sems((chips,)), sems((2 * APPLIES + 3, chips)),
-            sems((n_col,)), sems((2 * APPLIES + 2, n_col)),
+            sum_bufs(2), sum_bufs(1),
+            (vmem((2, BS, BS), f32), vmem((2, BS, BS), f32), vmem((2, width, width), f32),
+             vmem((2, BS, BS), f32), vmem((2, width, width), f32)),
+            sems((1,)), sems((APPLIES + 1,)),
+            sems((chips,)), sems((2 * APPLIES + 1, chips)),
+            sems((n_col,)), sems((2 * APPLIES + 1, n_col)),
             sems((chips,)), sems((APPLIES, chips)),
+            sems((1,)), sems((4,)),
+            sems((chips,)), sems((4, chips)),
+            sems((n_col,)), sems((2, n_col)),
         ],
         compiler_params=pltpu.CompilerParams(
             collective_id=0, has_side_effects=True, vmem_limit_bytes=60 * 1024 * 1024),
         interpret=interpret,
     )(table, blocks, start)
+
+
+def panels(s, e, lo, hi):
+    sub = lax.broadcasted_iota(jnp.int32, (8, BS), 0)
+    lane = lax.broadcasted_iota(jnp.int32, (8, BS), 1)
+
+    def panel(k, c):
+        first = pl.multiple_of(k * 8, 8)
+        for m in range(2):
+            r = s[m, pl.ds(first, 8), :]
+            g = e[m, pl.ds(first, 8), :]
+            own = jnp.where(lane >= first, jnp.where(lane < first + 8, r, 0.0), 0.0)
+            cols = []
+            for j in range(8):
+                at_j = jnp.where(lane == first + j, own, 0.0)
+                cols.append(jnp.broadcast_to(jnp.sum(at_j, axis=1, keepdims=True), (8, BS)))
+            scale = jnp.zeros((8, BS), f32)
+            for j in range(8):
+                pivot = jnp.broadcast_to(cols[j][j:j + 1], (8, BS))
+                mult = jnp.where(sub > j, cols[j] / pivot, 0.0)
+                scale = jnp.where(sub == j, pivot, scale)
+                r = r - mult * r[j:j + 1]
+                g = g - mult * g[j:j + 1]
+                for i in range(j + 1, 8):
+                    cols[i] = cols[i] - mult * cols[i][j:j + 1]
+            scale = 1.0 / jnp.sqrt(scale)
+            v = r * scale
+            g = g * scale
+            e[m, pl.ds(first, 8), :] = g
+            below = jnp.where(lane >= first + 8, v, 0.0)
+            step = lax.dot_general(below, jnp.concatenate([v, g], axis=1), (((0,), (0,)), ((), ())),
+                                   precision=highest, preferred_element_type=f32)
+            s[m] -= step[:, :BS]
+            e[m] -= step[:, BS:]
+        return c
+    lax.fori_loop(lo, hi, panel, 0)
 
 
 def local(block_values, block_index, block_count, start_vectors, interpret=False):
@@ -319,8 +424,6 @@
     chips = side * side
     blocks = block_values[0, 0]
     slots = blocks.shape[0]
-    width = start_vectors.shape[1]
-    total_rows = BS * n_row * n_col
     first, second = block_index[0, 0, 0], block_index[0, 0, 1]
     owner = second // n_col
     place = (first % n_col) * n_row + (owner % 2) * chips + owner // 2
@@ -329,21 +432,7 @@
     spots = jnp.arange(n_row * n_col, dtype=jnp.int32)
     table = jnp.sum(jnp.where(place[None, :] == spots[:, None], slot_ids[None, :] + 1, 0), axis=1)
 
-    vecs, grams = fused(table, blocks, start_vectors, side, n_col, interpret)
-    second_vec, third_vec = vecs[0], vecs[1]
-    grams = grams.transpose(2, 0, 1, 3, 4).reshape(3, width, width)
-    factors = jnp.linalg.cholesky(grams[:2])
-    inverses = jax.scipy.linalg.solve_triangular(
-        factors, jnp.broadcast_to(jnp.eye(width, dtype=f32), (2, width, width)), lower=True)
-    mul = functools.partial(jnp.matmul, precision=highest)
-    gram = mul(mul(inverses[0], grams[1]), inverses[0].T)
-    ritz = mul(mul(inverses[1], grams[2]), inverses[1].T)
-    subspace = mul(second_vec, inverses[1].T)
-    mapped = mul(third_vec, inverses[1].T)
-    gram_scaled = gram / jnp.sqrt(jnp.mean(gram * gram) + 1e-06)
-    spread = jnp.sqrt(jnp.mean(ritz * ritz) + 1e-06)
-    residual = (mapped - mul(subspace, ritz)) * (math.sqrt(total_rows / width) / spread)
-    return (subspace * math.sqrt(total_rows), ritz / spread, residual, gram_scaled)
+    return fused(table, blocks, start_vectors, side, n_col, interpret)
 
 
 def solution(mesh):

time: 332 us -> 203 us (0.61)
  other arithmetic: 110 us -> 1.46 us
  Pallas kernels: 207 us -> 193 us
  matrix products: 7.04 us -> 0 us
    another operation x14 -> x0, other arithmetic: 107 us -> none  [the longest x10 67.1 us: local(): factors = jnp.linalg.cholesky(grams[:2])]
    pallas_call x1, Pallas kernels: 207 us -> 193 us  [fused(): pl.pallas_call(functools.partial(kernel, side, n_col, width), out_shape=(...]
    unnamed x4, local copies, waits for them, and re-layouts: 0.01 us -> 6.47 us
    dot_general x7 -> x0, matrix products: 5.18 us -> none  [the longest x2 1.39 us: local(): ritz = mul(mul(inverses[1], grams[2]), inverses[1].T)]
    another operation x10 -> x0, local copies, waits for them, and re-layouts: 4.12 us -> none
where the time goes in v3:
time: 203 us
  Pallas kernels  193 us (95%)
  local copies, waits for them, and re-layouts  6.47 us (3%)
    pallas_call x1, Pallas kernels, fused(): pl.pallas_call(functools.partial(kernel, side, n_col, width), out_shape=(...  193 us
    unnamed x4, local copies, waits for them, and re-layouts  6.47 us

profile of v3, /device:TPU:1, one launch (start us, length us, event | category | flops | bytes accessed | tf_op | source)
XLA Modules:
  0.0 202.7 jit_solution(3404042902386734827)
XLA Ops:
  1.3 0.8 compare_select_fusion.2
  2.1 0.7 select_reduce_fusion.table
  2.7 193.4 %shard_map.75 = (f32[128,256]{1,0:T(8,128)}, f32[256,256]{1,0:T(8,128)}, f32[128,256]{1,0:T(8,128)}, f32[256,256]{1,0:T(8,128)}) custom-call(s32[256]{0:T(256)} %select_reduce_fusion.table, bf16[128,128,128]{2,1,0:T(8,128)(2,1)} %bitcast.17, f32[128,256]{1,0:T(8,128)} %start.1), custom_call_target="tpu_custom_call" | custom-call | tf_op jit(solution)/shard_map/pallas_call | solution.py:344
  196.2 1.6 copy.13
  197.8 1.7 copy.14
  199.4 1.6 copy.15
  201.0 1.7 copy.16

commit v4 on v3

v4 whole, which is shorter than its diff:
```python
import functools
import math

import jax
import jax.numpy as jnp
from jax import lax
from jax.experimental import pallas as pl
from jax.experimental.pallas import tpu as pltpu
from jax.sharding import PartitionSpec as P

APPLIES = 3
MESH = pl.DeviceIdType.MESH
highest = lax.Precision.HIGHEST
f32 = jnp.float32
bf16 = jnp.bfloat16
BS = 128


def kernel(side, n_col, width, table, stored, start, basis, projected, residual, scaled, scales,
           u, wt, wc, colp, colq, corep, rsend, rrecv, rowp, zsend, zrecv, yv, ytv,
           dacc, dcore, dxy, dz, gram_bufs, ritz_bufs, chol,
           s_core, r_core, s_xy, r_xy, s_z, r_z, s_fwd, r_fwd, s_rx, r_rx, s_rz, r_rz,
           t_core, q_core, t_xy, q_xy, t_z, q_z, blocks, b_sem):
    chips = side * side
    n_row = 2 * chips
    hw = width // 2
    row = lax.axis_index("row")
    z = lax.axis_index("col")
    core = lax.rem(row, 2)
    chip = row // 2
    y, x = chip // side, lax.rem(chip, side)
    other = 1 - core

    def sibling():
        return (chip * 2 + other, z)

    def xy_to(p):
        return lax.rem(y + p // side, side) * side + lax.rem(x + lax.rem(p, side), side)

    def xy_from(p):
        return lax.rem(y + side - p // side, side) * side + lax.rem(x + side - lax.rem(p, side), side)

    def z_to(p):
        return lax.rem(z + p, n_col)

    def z_from(p):
        return lax.rem(z + n_col - p, n_col)

    def xy_dev(t):
        return (t * 2 + core, z)

    def z_dev(t):
        return (row, t)

    def remote(src, dst, send, recv, dev):
        return pltpu.make_async_remote_copy(
            src_ref=src, dst_ref=dst, send_sem=send, recv_sem=recv,
            device_id=dev, device_id_type=MESH)

    def each(lo, hi, body, unroll=True):
        def step(i, c):
            body(i)
            return c
        lax.fori_loop(lo, hi, step, 0, unroll=unroll)

    load = pltpu.make_async_copy(stored, blocks, b_sem)
    load.start()

    barrier = pltpu.get_barrier_semaphore()
    pl.semaphore_signal(barrier, inc=1, device_id=sibling(), device_id_type=MESH)
    each(1, chips, lambda p: pl.semaphore_signal(
        barrier, inc=1, device_id=xy_dev(xy_to(p)), device_id_type=MESH))
    each(1, n_col, lambda p: pl.semaphore_signal(
        barrier, inc=1, device_id=z_dev(z_to(p)), device_id_type=MESH))

    dacc[...] = jnp.zeros_like(dacc)
    ones = jnp.ones((8, BS), f32)

    def fill_row(lr):
        def fill(pos, total):
            slot = table[lr * n_row + pos]
            live = (slot > 0).astype(f32)
            block = blocks[jnp.maximum(slot - 1, 0)].astype(f32) * live
            u[pl.ds(pl.multiple_of(lr * BS, BS), BS), pl.ds(pl.multiple_of(pos * BS, BS), BS)] = block.astype(bf16)
            size = jnp.abs(block)
            dacc[pos // chips, lax.rem(pos, chips)] += jnp.sum(size.reshape(BS // 8, 8, BS), axis=0)
            return total + size
        total = lax.fori_loop(0, n_row, fill, jnp.zeros((BS, BS), f32))
        rowp[0, lr, 0:8, 0:BS] = lax.dot_general(
            ones, total, (((1,), (1,)), ((), ())), precision=highest, preferred_element_type=f32)
    load.wait()
    each(0, n_col, fill_row, False)

    pl.semaphore_wait(barrier, 1 + (chips - 1) + (n_col - 1))

    D = APPLIES

    def deg_z(p, lr, slot):
        return remote(rowp.at[0, lr, 0:8, 0:BS], dz.at[p], s_z.at[p], r_z.at[D, p], z_dev(slot))
    each(1, n_col, lambda p: deg_z(p, z_to(p), z_to(p)).start())
    deg_core = remote(dacc.at[other], dcore, s_core.at[0], r_core.at[2 * D], sibling())
    deg_core.start()
    deg_core.wait()
    dacc[core] += dcore[...]

    def deg_xy(p):
        t = xy_to(p)
        return remote(dacc.at[core, t], dxy.at[p], s_xy.at[p], r_xy.at[D, p], xy_dev(t))
    each(1, chips, lambda p: deg_xy(p).start())
    dz[0] = rowp[0, z, 0:8, 0:BS]
    dxy[0] = dacc[core, chip]
    each(1, n_col, lambda p: deg_z(p, z_to(p), z_to(p)).wait())
    each(1, chips, lambda p: deg_xy(p).wait())
    degree = jnp.sum(dz[...], axis=0)[0:1] + jnp.sum(jnp.sum(dxy[...], axis=0), axis=0, keepdims=True)
    inv_row = 1.0 / jnp.sqrt(degree / BS + 1e-05)
    inv = jnp.broadcast_to(inv_row, (BS, BS)).T
    inv = inv[:, 0:1]
    yv[0] = start[...]

    def row_pos(k, t):
        return k * chips + t

    def apply_once(a, beside=lambda i: None):
        w = inv * yv[a]
        wc[(a % 2), pl.ds(pl.multiple_of(row_pos(core, chip) * BS, BS), BS), :] = w.astype(bf16)
        wt[a, :, pl.ds(pl.multiple_of(z * BS, BS), BS)] = w.T.astype(bf16)
        even = (a % 2)

        def wt_part(h, t):
            return wt.at[a, pl.ds(h * hw, hw), pl.ds(pl.multiple_of(t * BS, BS), BS)]

        def wc_part(h, k, t):
            return wc.at[even, pl.ds(pl.multiple_of(row_pos(k, t) * BS, BS), BS), pl.ds(h * hw, hw)]

        def z_send(h, p):
            part, i = wt_part(h, z), h * n_col + p
            return remote(part, part, s_z.at[i], r_z.at[a, i], z_dev(z_to(p)))

        def z_arrive(h, p):
            t, i = z_from(p), h * n_col + p
            return remote(wt_part(h, t), wt_part(h, t), s_z.at[i], r_z.at[a, i], z_dev(t))

        def xy_send(h, p):
            part, i = wc_part(h, core, chip), h * chips + p
            return remote(part, part, s_xy.at[i], r_xy.at[a, i], xy_dev(xy_to(p)))

        def xy_arrive(h, p):
            t, i = xy_from(p), h * chips + p
            return remote(wc_part(h, core, t), wc_part(h, core, t), s_xy.at[i], r_xy.at[a, i], xy_dev(t))

        def pass_on(h, k, p):
            t, i = xy_from(p), h * chips + p
            return remote(wc_part(h, k, t), wc_part(h, k, t), s_fwd.at[i], r_fwd.at[a, i], sibling())

        def swap(h):
            return remote(colq.at[h], corep.at[a, h], s_core.at[h], r_core.at[a * 2 + h], sibling())

        def rs_xy(h, p):
            i = h * chips + p
            return remote(rsend.at[h, p], rrecv.at[a, h, p], s_rx.at[i], r_rx.at[a, i], xy_dev(xy_to(p)))

        def rs_z(h, p):
            i = h * n_col + p
            return remote(zsend.at[h, p], zrecv.at[a, h, p], s_rz.at[i], r_rz.at[a, i], z_dev(z_to(p)))

        def send_out(h):
            each(1, n_col, lambda p: z_send(h, p).start())
            each(1, chips, lambda p: xy_send(h, p).start())
            pass_on(h, core, 0).start()

        send_out(0)
        beside(0)

        def col_tiles(h, k, out_ref):
            def tile(n):
                first = (k * chips + 2 * n) * BS
                out = jnp.dot(wt[a, h * hw:(h + 1) * hw, :], u[:, pl.ds(pl.multiple_of(first, 2 * BS), 2 * BS)],
                              preferred_element_type=f32)
                out_ref[h, 2 * n] = out[:, :BS].astype(out_ref.dtype)
                out_ref[h, 2 * n + 1] = out[:, BS:].astype(out_ref.dtype)
            each(0, chips // 2, tile)

        for h in range(2):
            each(1, n_col, lambda p: z_arrive(h, p).wait_recv())
            if h == 0:
                send_out(1)
                beside(1)
            col_tiles(h, other, colq)
            swap(h).start()
            col_tiles(h, core, colp)

            def relay(p):
                xy_arrive(h, p).wait_recv()
                pass_on(h, core, p).start()
            each(1, chips, relay)
            if h == 0:
                beside(2)
            swap(h).wait_recv()

            def combine(p):
                t = xy_to(p)
                rsend[h, p] = (colp[h, t] + corep[a, h, t].astype(f32)).astype(bf16)
                rs_xy(h, p).start()
            each(1, chips, combine)
            each(0, chips, lambda p: pass_on(h, other, p).wait_recv())

            def row_tile(n):
                out = jnp.dot(u[pl.ds(pl.multiple_of(n * 2 * BS, 2 * BS), 2 * BS), :],
                              wc[even, :, h * hw:(h + 1) * hw], preferred_element_type=f32)
                rowp[h, 2 * n] = out[:BS]
                rowp[h, 2 * n + 1] = out[BS:]
            each(0, n_col // 2, row_tile)

            def row_go(p):
                zsend[h, p] = rowp[h, z_to(p)].astype(bf16)
                rs_z(h, p).start()
            each(1, n_col, row_go)
            beside(3 + h)

        for h in range(2):
            def add_col(p, total):
                rs_xy(h, p).wait_recv()
                return total + rrecv[a, h, p].astype(f32)
            cols = lax.fori_loop(1, chips, add_col, colp[h, chip] + corep[a, h, chip].astype(f32))

            def add_row(p, total):
                rs_z(h, p).wait_recv()
                return total + zrecv[a, h, p].astype(f32)
            rows = lax.fori_loop(1, n_col, add_row, rowp[h, z])
            out = inv * (rows + cols.T)
            yv[a + 1, :, h * hw:(h + 1) * hw] = out
            ytv[a, h * hw:(h + 1) * hw, :] = out.T
        for h in range(2):
            swap(h).wait_send()

            def xy_sent(p):
                xy_send(h, p).wait_send()
                rs_xy(h, p).wait_send()
            each(1, chips, xy_sent)

            def z_sent(p):
                z_send(h, p).wait_send()
                rs_z(h, p).wait_send()
            each(1, n_col, z_sent)
            each(0, chips, lambda p: pass_on(h, core, p).wait_send())

    def local_gram(a, b, into, n):
        g = jnp.dot(ytv[a], yv[b], precision=highest, preferred_element_type=f32)
        g = g.reshape(2, chips, width // n_row, width)
        for k in range(2):
            for t in range(chips):
                into[k, t, n] = g[k, t]

    def sum_steps(bufs, base):
        gr, ga, gb, gc, gd = bufs
        q = 2 * base
        g_core = remote(gr.at[other], ga, t_core.at[0], q_core.at[q], sibling())
        g_last = remote(gd.at[core], gd.at[core], t_core.at[0], q_core.at[q + 1], sibling())

        def g_xy(p):
            t = xy_to(p)
            return remote(gr.at[core, t], gb.at[p], t_xy.at[p], q_xy.at[q, p], xy_dev(t))

        def g_z(p):
            return remote(gc.at[0], gc.at[p], t_z.at[p], q_z.at[base, p], z_dev(z_to(p)))

        def g_back(p):
            t = xy_from(p)
            return remote(gd.at[core, t], gd.at[core, t], t_xy.at[p], q_xy.at[q + 1, p], xy_dev(t))

        def g_out(p):
            return remote(gd.at[core, chip], gd.at[core, chip], t_xy.at[p], q_xy.at[q + 1, p], xy_dev(xy_to(p)))

        def add_z(t, total):
            return total + gc[lax.rem(z + n_col - t, n_col)]

        def step1():
            g_core.wait()
            gr[core] += ga[...]
            each(1, chips, lambda p: g_xy(p).start())

        def step2():
            each(1, chips, lambda p: g_xy(p).wait())
            gb[0] = gr[core, chip]
            gc[0] = jnp.sum(gb[...], axis=0)
            each(1, n_col, lambda p: g_z(p).start())

        def step3():
            each(1, n_col, lambda p: g_z(p).wait())
            gd[core, chip] = lax.fori_loop(1, n_col, add_z, gc[z])
            each(1, chips, lambda p: g_out(p).start())

        def step4():
            each(1, chips, lambda p: g_back(p).wait_recv())
            each(1, chips, lambda p: g_out(p).wait_send())
            g_last.start()

        def step5():
            g_last.wait_send()
            remote(gd.at[other], gd.at[other], t_core.at[0], q_core.at[q + 1], sibling()).wait_recv()

        return g_core.start, step1, step2, step3, step4, step5

    mul = functools.partial(jnp.dot, precision=highest, preferred_element_type=f32)
    tmul = lambda a, b: lax.dot_general(a, b, (((0,), (0,)), ((), ())), precision=highest, preferred_element_type=f32)
    s, e, li, half, full = chol

    gram_sum = sum_steps(gram_bufs, 0)

    def last_apply(i):
        if i == 0:
            local_gram(0, 1, gram_bufs[0], 0)
            local_gram(1, 2, gram_bufs[0], 1)
            gram_sum[0]()
            gram_sum[1]()
        else:
            gram_sum[i + 1]()
        if i == 4:
            first_factors()

    def first_factors():
        for m in range(2):
            full[m] = gram_bufs[4][:, :, m].reshape(width, width)
            s[m] = full[m, :BS, :BS]
        unit(e)
        panels(s, e, 0, BS // 8)
        for m in range(2):
            li[m, :BS, :BS] = e[m]
            li[m, :BS, BS:] = jnp.zeros((BS, BS), f32)
            half[m] = mul(e[m], full[m, :BS, BS:])
            s[m] = full[m, BS:, BS:] - tmul(half[m], half[m])
        unit(e)

    each(0, APPLIES - 1, apply_once, False)
    apply_once(APPLIES - 1, last_apply)
    local_gram(1, 3, ritz_bufs[0], 0)
    cuts = (0, 2, 7, 11, 16)

    def second_factors(i):
        if i < 4:
            panels(s, e, cuts[i], cuts[i + 1])
        else:
            for m in range(2):
                li[m, BS:, BS:] = e[m]
                li[m, BS:, :BS] = -mul(e[m], tmul(half[m], li[m, :BS, :BS]))
            gram = mul(mul(li[0], full[1]), li[0].T)
            scaled[...] = gram
            scales[1] = jnp.broadcast_to(
                1.0 / jnp.sqrt(jnp.sum(gram * gram, keepdims=True) / (width * width) + 1e-06), (8, BS))
            full[0] = li[1].T
            yv[0] = mul(yv[2], full[0])
            yv[1] = mul(yv[3], full[0])

    ritz_sum = sum_steps(ritz_bufs, 1)
    for i in range(5):
        ritz_sum[i]()
        second_factors(i)
    ritz_sum[5]()
    ritz = mul(mul(li[1], ritz_bufs[4][:, :, 0].reshape(width, width)), full[0])
    scales[0] = jnp.broadcast_to(1.0 / jnp.sqrt(jnp.sum(ritz * ritz, keepdims=True) / (width * width) + 1e-06), (8, BS))
    projected[...] = ritz
    basis[...] = yv[0]
    residual[...] = yv[1] - mul(yv[0], ritz)


def unit(e):
    eye = (lax.broadcasted_iota(jnp.int32, (BS, BS), 0) == lax.broadcasted_iota(jnp.int32, (BS, BS), 1)).astype(f32)
    for m in range(2):
        e[m] = eye


def fused(table, blocks, start, side, n_col, interpret=False):
    chips = side * side
    n_row = 2 * chips
    width = start.shape[1]
    sems = pltpu.SemaphoreType.DMA
    vmem = pltpu.VMEM
    part = width // n_row
    hw = width // 2
    tall = jax.ShapeDtypeStruct((BS, width), f32)
    square = jax.ShapeDtypeStruct((width, width), f32)

    def sum_bufs(n):
        return (vmem((2, chips, n, part, width), f32), vmem((chips, n, part, width), f32),
                vmem((chips, n, part, width), f32), vmem((n_col, n, part, width), f32),
                vmem((2, chips, n, part, width), f32))
    return pl.pallas_call(
        functools.partial(kernel, side, n_col, width),
        out_shape=(tall, square, tall, square, jax.ShapeDtypeStruct((2, 8, BS), f32)),
        in_specs=[pl.BlockSpec(memory_space=pltpu.SMEM), pl.BlockSpec(memory_space=pl.ANY), pl.BlockSpec(memory_space=pltpu.VMEM)],
        out_specs=tuple([pl.BlockSpec(memory_space=pltpu.VMEM)] * 5),
        scratch_shapes=[
            vmem((n_col * BS, n_row * BS), bf16),
            vmem((APPLIES, width, n_col * BS), bf16),
            vmem((2, n_row * BS, width), bf16),
            vmem((2, chips, hw, BS), f32),
            vmem((2, chips, hw, BS), bf16),
            vmem((APPLIES, 2, chips, hw, BS), bf16),
            vmem((2, chips, hw, BS), bf16),
            vmem((APPLIES, 2, chips, hw, BS), bf16),
            vmem((2, n_col, BS, hw), f32),
            vmem((2, n_col, BS, hw), bf16),
            vmem((APPLIES, 2, n_col, BS, hw), bf16),
            vmem((APPLIES + 1, BS, width), f32),
            vmem((APPLIES, width, BS), f32),
            vmem((2, chips, 8, BS), f32),
            vmem((chips, 8, BS), f32),
            vmem((chips, 8, BS), f32),
            vmem((n_col, 8, BS), f32),
            sum_bufs(2), sum_bufs(1),
            (vmem((2, BS, BS), f32), vmem((2, BS, BS), f32), vmem((2, width, width), f32),
             vmem((2, BS, BS), f32), vmem((2, width, width), f32)),
            sems((2,)), sems((2 * APPLIES + 1,)),
            sems((2 * chips,)), sems((APPLIES + 1, 2 * chips)),
            sems((2 * n_col,)), sems((APPLIES + 1, 2 * n_col)),
            sems((2 * chips,)), sems((APPLIES, 2 * chips)),
            sems((2 * chips,)), sems((APPLIES, 2 * chips)),
            sems((2 * n_col,)), sems((APPLIES, 2 * n_col)),
            sems((1,)), sems((4,)),
            sems((chips,)), sems((4, chips)),
            sems((n_col,)), sems((2, n_col)),
            vmem(blocks.shape, bf16), sems(()),
        ],
        compiler_params=pltpu.CompilerParams(
            collective_id=0, has_side_effects=True, vmem_limit_bytes=60 * 1024 * 1024),
        interpret=interpret,
    )(table, blocks, start)


def panels(s, e, lo, hi):
    sub = lax.broadcasted_iota(jnp.int32, (8, BS), 0)
    lane = lax.broadcasted_iota(jnp.int32, (8, BS), 1)

    def panel(k, c):
        first = pl.multiple_of(k * 8, 8)
        for m in range(2):
            r = s[m, pl.ds(first, 8), :]
            g = e[m, pl.ds(first, 8), :]
            own = jnp.where(lane >= first, jnp.where(lane < first + 8, r, 0.0), 0.0)
            cols = []
            for j in range(8):
                at_j = jnp.where(lane == first + j, own, 0.0)
                cols.append(jnp.broadcast_to(jnp.sum(at_j, axis=1, keepdims=True), (8, BS)))
            scale = jnp.zeros((8, BS), f32)
            for j in range(8):
                pivot = jnp.broadcast_to(cols[j][j:j + 1], (8, BS))
                mult = jnp.where(sub > j, cols[j] / pivot, 0.0)
                scale = jnp.where(sub == j, pivot, scale)
                r = r - mult * r[j:j + 1]
                g = g - mult * g[j:j + 1]
                for i in range(j + 1, 8):
                    cols[i] = cols[i] - mult * cols[i][j:j + 1]
            scale = 1.0 / jnp.sqrt(scale)
            v = r * scale
            g = g * scale
            e[m, pl.ds(first, 8), :] = g
            below = jnp.where(lane >= first + 8, v, 0.0)
            step = lax.dot_general(below, jnp.concatenate([v, g], axis=1), (((0,), (0,)), ((), ())),
                                   precision=highest, preferred_element_type=f32)
            s[m] -= step[:, :BS]
            e[m] -= step[:, BS:]
        return c
    lax.fori_loop(lo, hi, panel, 0)


def local(block_values, block_index, block_count, start_vectors, interpret=False):
    n_row = lax.axis_size("row")
    n_col = lax.axis_size("col")
    side = math.isqrt(n_row // 2)
    chips = side * side
    blocks = block_values[0, 0]
    slots = blocks.shape[0]
    first, second = block_index[0, 0, 0], block_index[0, 0, 1]
    owner = second // n_col
    place = (first % n_col) * n_row + (owner % 2) * chips + owner // 2
    slot_ids = jnp.arange(slots, dtype=jnp.int32)
    place = jnp.where(slot_ids < block_count[0, 0], place, -1)
    spots = jnp.arange(n_row * n_col, dtype=jnp.int32)
    table = jnp.sum(jnp.where(place[None, :] == spots[:, None], slot_ids[None, :] + 1, 0), axis=1)

    parts = fused(table, blocks, start_vectors, side, n_col, interpret)
    total_rows = BS * n_row * n_col
    whole = pl.BlockSpec(memory_space=pltpu.VMEM)
    return pl.pallas_call(
        functools.partial(scale_kernel, math.sqrt(total_rows), math.sqrt(total_rows / start_vectors.shape[1])),
        out_shape=tuple(jax.ShapeDtypeStruct(p.shape, f32) for p in parts[:4]),
        in_specs=[whole] * 5,
        out_specs=(whole,) * 4,
        interpret=interpret,
    )(*parts)


def scale_kernel(tall, rest, subspace, ritz, residual, gram, scales, basis, projected, ritz_residual, gram_scaled):
    inverse_spread, inverse_size = scales[0, 0:1, 0:1], scales[1, 0:1, 0:1]
    basis[...] = subspace[...] * tall
    projected[...] = ritz[...] * inverse_spread
    ritz_residual[...] = residual[...] * (inverse_spread * rest)
    gram_scaled[...] = gram[...] * inverse_size


def solution(mesh):
    return jax.shard_map(
        local,
        mesh=mesh,
        in_specs=(
            P("row", "col", None, None, None),
            P("row", "col", None, None),
            P("row", "col"),
            P(("row", "col"), None),
        ),
        out_specs=(P(("row", "col"), None), P(), P(("row", "col"), None), P()),
        check_vma=False,
    )
```

time: 203 us -> 177 us (0.87)
  Pallas kernels: 193 us -> 174 us
  local copies, waits for them, and re-layouts: 6.47 us -> 0 us
    pallas_call x1, Pallas kernels: 193 us -> 172 us  [fused(): pl.pallas_call(functools.partial(kernel, side, n_col, width), out_shape=(...]
    unnamed x4 -> x0, local copies, waits for them, and re-layouts: 6.47 us -> none
where the time goes in v4:
time: 177 us
  Pallas kernels  174 us (98%)
    pallas_call x1, Pallas kernels, fused(): pl.pallas_call(functools.partial(kernel, side, n_col, width), out_shape=(...  172 us

profile of v4, /device:TPU:1, one launch (start us, length us, event | category | flops | bytes accessed | tf_op | source)
XLA Modules:
  0.0 176.6 jit_solution(5647401208210653574)
XLA Ops:
  1.3 0.8 compare_select_fusion.2
  2.1 0.7 select_reduce_fusion.table
  2.7 171.8 %shard_map.75 = (f32[128,256]{1,0:T(8,128)}, f32[256,256]{1,0:T(8,128)}, f32[128,256]{1,0:T(8,128)}, f32[256,256]{1,0:T(8,128)}, f32[2,8,128]{2,1,0:T(8,128)}) custom-call(s32[256]{0:T(256)} %select_reduce_fusion.table, bf16[128,128,128]{2,1,0:T(8,128)(2,1)} %bitcast.17, f32[128,256]{1,0:T(8,128)} %start.1), custom_call_target="tpu_custom_call" | custom-call | tf_op jit(solution)/shard_map/pallas_call | solution.py:387
  174.6 2.0 %shard_map.76 = (f32[128,256]{1,0:T(8,128)}, f32[256,256]{1,0:T(8,128)}, f32[128,256]{1,0:T(8,128)}, f32[256,256]{1,0:T(8,128)}) custom-call(f32[128,256]{1,0:T(8,128)} %get-tuple-element.9.subspace, f32[256,256]{1,0:T(8,128)} %get-tuple-element.10.ritz, f32[128,256]{1,0:T(8,128)} %get-tuple-element.11.residual, f32[256,256]{1,0:T(8,128)} %get-tuple-element.12.gram, ...), custom_call_target="tpu_custom_call" | custom-call | tf_op jit(solution)/shard_map/pallas_call | solution.py:484

commit v5 on v4

--- a/solution.py
+++ b/solution.py
@@ -96,7 +96,7 @@
     D = APPLIES
 
     def deg_z(p, lr, slot):
-        return remote(rowp.at[0, lr, 0:8, 0:BS], dz.at[p], s_z.at[p], r_z.at[D, p], z_dev(slot))
+        return remote(rowp.at[0, lr, 0:8, 0:BS], dz.at[p], s_z.at[0], r_z.at[D, 0], z_dev(slot))
     each(1, n_col, lambda p: deg_z(p, z_to(p), z_to(p)).start())
     deg_core = remote(dacc.at[other], dcore, s_core.at[0], r_core.at[2 * D], sibling())
     deg_core.start()
@@ -105,12 +105,12 @@
 
     def deg_xy(p):
         t = xy_to(p)
-        return remote(dacc.at[core, t], dxy.at[p], s_xy.at[p], r_xy.at[D, p], xy_dev(t))
+        return remote(dacc.at[core, t], dxy.at[p], s_xy.at[0], r_xy.at[D, 0], xy_dev(t))
     each(1, chips, lambda p: deg_xy(p).start())
     dz[0] = rowp[0, z, 0:8, 0:BS]
     dxy[0] = dacc[core, chip]
-    each(1, n_col, lambda p: deg_z(p, z_to(p), z_to(p)).wait())
-    each(1, chips, lambda p: deg_xy(p).wait())
+    remote(dz.at[1:], dz.at[1:], s_z.at[0], r_z.at[D, 0], z_dev(z_to(1))).wait()
+    remote(dxy.at[1:], dxy.at[1:], s_xy.at[0], r_xy.at[D, 0], xy_dev(xy_to(1))).wait()
     degree = jnp.sum(dz[...], axis=0)[0:1] + jnp.sum(jnp.sum(dxy[...], axis=0), axis=0, keepdims=True)
     inv_row = 1.0 / jnp.sqrt(degree / BS + 1e-05)
     inv = jnp.broadcast_to(inv_row, (BS, BS)).T
@@ -133,40 +133,41 @@
             return wc.at[even, pl.ds(pl.multiple_of(row_pos(k, t) * BS, BS), BS), pl.ds(h * hw, hw)]
 
         def z_send(h, p):
-            part, i = wt_part(h, z), h * n_col + p
-            return remote(part, part, s_z.at[i], r_z.at[a, i], z_dev(z_to(p)))
-
-        def z_arrive(h, p):
-            t, i = z_from(p), h * n_col + p
-            return remote(wt_part(h, t), wt_part(h, t), s_z.at[i], r_z.at[a, i], z_dev(t))
+            return remote(wt_part(h, z), wt_part(h, z), s_z.at[h], r_z.at[a, h], z_dev(z_to(p)))
 
         def xy_send(h, p):
-            part, i = wc_part(h, core, chip), h * chips + p
-            return remote(part, part, s_xy.at[i], r_xy.at[a, i], xy_dev(xy_to(p)))
-
-        def xy_arrive(h, p):
-            t, i = xy_from(p), h * chips + p
-            return remote(wc_part(h, core, t), wc_part(h, core, t), s_xy.at[i], r_xy.at[a, i], xy_dev(t))
-
-        def pass_on(h, k, p):
-            t, i = xy_from(p), h * chips + p
-            return remote(wc_part(h, k, t), wc_part(h, k, t), s_fwd.at[i], r_fwd.at[a, i], sibling())
+            part = wc_part(h, core, chip)
+            return remote(part, part, s_xy.at[h], r_xy.at[a, h], xy_dev(xy_to(p)))
+
+        def z_all(h):
+            return remote(zsend.at[h, 1:], zrecv.at[a, h, 1:], s_z.at[h], r_z.at[a, h], z_dev(z_to(1)))
+
+        def xy_all(h):
+            return remote(rsend.at[h, 1:], rrecv.at[a, h, 1:], s_xy.at[h], r_xy.at[a, h], xy_dev(xy_to(1)))
+
+        def rs_z_all(h):
+            return remote(zsend.at[h, 1:], zrecv.at[a, h, 1:], s_rz.at[h], r_rz.at[a, h], z_dev(z_to(1)))
+
+        def rs_xy_all(h):
+            return remote(rsend.at[h, 1:], rrecv.at[a, h, 1:], s_rx.at[h], r_rx.at[a, h], xy_dev(xy_to(1)))
+
+        def pass_on(h, k, g):
+            first = row_pos(k, g * side) * BS
+            part = wc.at[even, pl.ds(pl.multiple_of(first, BS), side * BS), pl.ds(h * hw, hw)]
+            return remote(part, part, s_fwd.at[h, g], r_fwd.at[a, h * side + g], sibling())
 
         def swap(h):
             return remote(colq.at[h], corep.at[a, h], s_core.at[h], r_core.at[a * 2 + h], sibling())
 
         def rs_xy(h, p):
-            i = h * chips + p
-            return remote(rsend.at[h, p], rrecv.at[a, h, p], s_rx.at[i], r_rx.at[a, i], xy_dev(xy_to(p)))
+            return remote(rsend.at[h, p], rrecv.at[a, h, p], s_rx.at[h], r_rx.at[a, h], xy_dev(xy_to(p)))
 
         def rs_z(h, p):
-            i = h * n_col + p
-            return remote(zsend.at[h, p], zrecv.at[a, h, p], s_rz.at[i], r_rz.at[a, i], z_dev(z_to(p)))
+            return remote(zsend.at[h, p], zrecv.at[a, h, p], s_rz.at[h], r_rz.at[a, h], z_dev(z_to(p)))
 
         def send_out(h):
             each(1, n_col, lambda p: z_send(h, p).start())
             each(1, chips, lambda p: xy_send(h, p).start())
-            pass_on(h, core, 0).start()
 
         send_out(0)
         beside(0)
@@ -181,18 +182,15 @@
             each(0, chips // 2, tile)
 
         for h in range(2):
-            each(1, n_col, lambda p: z_arrive(h, p).wait_recv())
+            z_all(h).wait_recv()
             if h == 0:
                 send_out(1)
                 beside(1)
             col_tiles(h, other, colq)
             swap(h).start()
             col_tiles(h, core, colp)
-
-            def relay(p):
-                xy_arrive(h, p).wait_recv()
-                pass_on(h, core, p).start()
-            each(1, chips, relay)
+            xy_all(h).wait_recv()
+            each(0, side, lambda g: pass_on(h, core, g).start())
             if h == 0:
                 beside(2)
             swap(h).wait_recv()
@@ -202,7 +200,7 @@
                 rsend[h, p] = (colp[h, t] + corep[a, h, t].astype(f32)).astype(bf16)
                 rs_xy(h, p).start()
             each(1, chips, combine)
-            each(0, chips, lambda p: pass_on(h, other, p).wait_recv())
+            each(0, side, lambda g: pass_on(h, other, g).wait_recv())
 
             def row_tile(n):
                 out = jnp.dot(u[pl.ds(pl.multiple_of(n * 2 * BS, 2 * BS), 2 * BS), :],
@@ -218,31 +216,22 @@
             beside(3 + h)
 
         for h in range(2):
-            def add_col(p, total):
-                rs_xy(h, p).wait_recv()
-                return total + rrecv[a, h, p].astype(f32)
-            cols = lax.fori_loop(1, chips, add_col, colp[h, chip] + corep[a, h, chip].astype(f32))
-
-            def add_row(p, total):
-                rs_z(h, p).wait_recv()
-                return total + zrecv[a, h, p].astype(f32)
-            rows = lax.fori_loop(1, n_col, add_row, rowp[h, z])
+            rs_xy_all(h).wait_recv()
+            cols = colp[h, chip] + corep[a, h, chip].astype(f32)
+            for p in range(1, chips):
+                cols = cols + rrecv[a, h, p].astype(f32)
+            rs_z_all(h).wait_recv()
+            rows = rowp[h, z]
+            for p in range(1, n_col):
+                rows = rows + zrecv[a, h, p].astype(f32)
             out = inv * (rows + cols.T)
             yv[a + 1, :, h * hw:(h + 1) * hw] = out
             ytv[a, h * hw:(h + 1) * hw, :] = out.T
         for h in range(2):
             swap(h).wait_send()
-
-            def xy_sent(p):
-                xy_send(h, p).wait_send()
-                rs_xy(h, p).wait_send()
-            each(1, chips, xy_sent)
-
-            def z_sent(p):
-                z_send(h, p).wait_send()
-                rs_z(h, p).wait_send()
-            each(1, n_col, z_sent)
-            each(0, chips, lambda p: pass_on(h, core, p).wait_send())
+            for copies in (z_all(h), xy_all(h), rs_z_all(h), rs_xy_all(h)):
+                copies.wait_send()
+            each(0, side, lambda g: pass_on(h, core, g).wait_send())
 
     def local_gram(a, b, into, n):
         g = jnp.dot(ytv[a], yv[b], precision=highest, preferred_element_type=f32)
@@ -259,17 +248,16 @@
 
         def g_xy(p):
             t = xy_to(p)
-            return remote(gr.at[core, t], gb.at[p], t_xy.at[p], q_xy.at[q, p], xy_dev(t))
+            return remote(gr.at[core, t], gb.at[p], t_xy.at[q], q_xy.at[q], xy_dev(t))
 
         def g_z(p):
-            return remote(gc.at[0], gc.at[p], t_z.at[p], q_z.at[base, p], z_dev(z_to(p)))
-
-        def g_back(p):
-            t = xy_from(p)
-            return remote(gd.at[core, t], gd.at[core, t], t_xy.at[p], q_xy.at[q + 1, p], xy_dev(t))
+            return remote(gc.at[0], gc.at[p], t_z.at[base], q_z.at[base], z_dev(z_to(p)))
+
+        def all_xy(k):
+            return remote(ga.at[1:], gb.at[1:], t_xy.at[k], q_xy.at[k], xy_dev(xy_to(1)))
 
         def g_out(p):
-            return remote(gd.at[core, chip], gd.at[core, chip], t_xy.at[p], q_xy.at[q + 1, p], xy_dev(xy_to(p)))
+            return remote(gd.at[core, chip], gd.at[core, chip], t_xy.at[q + 1], q_xy.at[q + 1], xy_dev(xy_to(p)))
 
         def add_z(t, total):
             return total + gc[lax.rem(z + n_col - t, n_col)]
@@ -280,19 +268,18 @@
             each(1, chips, lambda p: g_xy(p).start())
 
         def step2():
-            each(1, chips, lambda p: g_xy(p).wait())
+            all_xy(q).wait()
             gb[0] = gr[core, chip]
             gc[0] = jnp.sum(gb[...], axis=0)
             each(1, n_col, lambda p: g_z(p).start())
 
         def step3():
-            each(1, n_col, lambda p: g_z(p).wait())
+            remote(gc.at[1:], gc.at[1:], t_z.at[base], q_z.at[base], z_dev(z_to(1))).wait()
             gd[core, chip] = lax.fori_loop(1, n_col, add_z, gc[z])
             each(1, chips, lambda p: g_out(p).start())
 
         def step4():
-            each(1, chips, lambda p: g_back(p).wait_recv())
-            each(1, chips, lambda p: g_out(p).wait_send())
+            all_xy(q + 1).wait()
             g_last.start()
 
         def step5():
@@ -411,14 +398,14 @@
             (vmem((2, BS, BS), f32), vmem((2, BS, BS), f32), vmem((2, width, width), f32),
              vmem((2, BS, BS), f32), vmem((2, width, width), f32)),
             sems((2,)), sems((2 * APPLIES + 1,)),
-            sems((2 * chips,)), sems((APPLIES + 1, 2 * chips)),
-            sems((2 * n_col,)), sems((APPLIES + 1, 2 * n_col)),
-            sems((2 * chips,)), sems((APPLIES, 2 * chips)),
-            sems((2 * chips,)), sems((APPLIES, 2 * chips)),
-            sems((2 * n_col,)), sems((APPLIES, 2 * n_col)),
+            sems((2,)), sems((APPLIES + 1, 2)),
+            sems((2,)), sems((APPLIES + 1, 2)),
+            sems((2, side)), sems((APPLIES, 2 * side)),
+            sems((2,)), sems((APPLIES, 2)),
+            sems((2,)), sems((APPLIES, 2)),
             sems((1,)), sems((4,)),
-            sems((chips,)), sems((4, chips)),
-            sems((n_col,)), sems((2, n_col)),
+            sems((4,)), sems((4,)),
+            sems((2,)), sems((2,)),
             vmem(blocks.shape, bf16), sems(()),
         ],
         compiler_params=pltpu.CompilerParams(

time: 177 us -> 170 us (0.960)
  Pallas kernels: 174 us -> 167 us
    pallas_call x1, Pallas kernels: 172 us -> 165 us  [fused(): pl.pallas_call(functools.partial(kernel, side, n_col, width), out_shape=(...]
where the time goes in v5:
time: 170 us
  Pallas kernels  167 us (98%)
    pallas_call x1, Pallas kernels, fused(): pl.pallas_call(functools.partial(kernel, side, n_col, width), out_shape=(...  165 us

profile of v5, /device:TPU:1, one launch (start us, length us, event | category | flops | bytes accessed | tf_op | source)
XLA Modules:
  0.0 169.9 jit_solution(18289883458390587928)
XLA Ops:
  1.3 0.8 compare_select_fusion.2
  2.1 0.7 select_reduce_fusion.table
  2.7 165.2 %shard_map.75 = (f32[128,256]{1,0:T(8,128)}, f32[256,256]{1,0:T(8,128)}, f32[128,256]{1,0:T(8,128)}, f32[256,256]{1,0:T(8,128)}, f32[2,8,128]{2,1,0:T(8,128)}) custom-call(s32[256]{0:T(256)} %select_reduce_fusion.table, bf16[128,128,128]{2,1,0:T(8,128)(2,1)} %bitcast.17, f32[128,256]{1,0:T(8,128)} %start.1), custom_call_target="tpu_custom_call" | custom-call | tf_op jit(solution)/shard_map/pallas_call | solution.py:374
  167.9 2.0 %shard_map.76 = (f32[128,256]{1,0:T(8,128)}, f32[256,256]{1,0:T(8,128)}, f32[128,256]{1,0:T(8,128)}, f32[256,256]{1,0:T(8,128)}) custom-call(f32[128,256]{1,0:T(8,128)} %get-tuple-element.9.subspace, f32[256,256]{1,0:T(8,128)} %get-tuple-element.10.ritz, f32[128,256]{1,0:T(8,128)} %get-tuple-element.11.residual, f32[256,256]{1,0:T(8,128)} %get-tuple-element.12.gram, ...), custom_call_target="tpu_custom_call" | custom-call | tf_op jit(solution)/shard_map/pallas_call | solution.py:471

commit v6 on v5

--- a/solution.py
+++ b/solution.py
@@ -170,6 +170,7 @@
             each(1, chips, lambda p: xy_send(h, p).start())
 
         send_out(0)
+        send_out(1)
         beside(0)
 
         def col_tiles(h, k, out_ref):
@@ -184,7 +185,6 @@
         for h in range(2):
             z_all(h).wait_recv()
             if h == 0:
-                send_out(1)
                 beside(1)
             col_tiles(h, other, colq)
             swap(h).start()
@@ -442,10 +442,13 @@
             g = g * scale
             e[m, pl.ds(first, 8), :] = g
             below = jnp.where(lane >= first + 8, v, 0.0)
-            step = lax.dot_general(below, jnp.concatenate([v, g], axis=1), (((0,), (0,)), ((), ())),
-                                   precision=highest, preferred_element_type=f32)
-            s[m] -= step[:, :BS]
-            e[m] -= step[:, BS:]
+            below = below.T
+            trail, inverse = s[m], e[m]
+            for j in range(8):
+                trail = trail - below[:, j:j + 1] * v[j:j + 1]
+                inverse = inverse - below[:, j:j + 1] * g[j:j + 1]
+            s[m] = trail
+            e[m] = inverse
         return c
     lax.fori_loop(lo, hi, panel, 0)
 

time: 170 us -> 165 us (0.971)
  Pallas kernels: 167 us -> 162 us
    pallas_call x1, Pallas kernels: 165 us -> 160 us  [fused(): pl.pallas_call(functools.partial(kernel, side, n_col, width), out_shape=(...]
where the time goes in v6:
time: 165 us
  Pallas kernels  162 us (98%)
    pallas_call x1, Pallas kernels, fused(): pl.pallas_call(functools.partial(kernel, side, n_col, width), out_shape=(...  160 us

profile of v6, /device:TPU:1, one launch (start us, length us, event | category | flops | bytes accessed | tf_op | source)
XLA Modules:
  0.0 165.0 jit_solution(6645646999879520404)
XLA Ops:
  1.3 0.8 compare_select_fusion.2
  2.1 0.7 select_reduce_fusion.table
  2.7 160.3 %shard_map.75 = (f32[128,256]{1,0:T(8,128)}, f32[256,256]{1,0:T(8,128)}, f32[128,256]{1,0:T(8,128)}, f32[256,256]{1,0:T(8,128)}, f32[2,8,128]{2,1,0:T(8,128)}) custom-call(s32[256]{0:T(256)} %select_reduce_fusion.table, bf16[128,128,128]{2,1,0:T(8,128)(2,1)} %bitcast.17, f32[128,256]{1,0:T(8,128)} %start.1), custom_call_target="tpu_custom_call" | custom-call | tf_op jit(solution)/shard_map/pallas_call | solution.py:374
  163.0 2.0 %shard_map.76 = (f32[128,256]{1,0:T(8,128)}, f32[256,256]{1,0:T(8,128)}, f32[128,256]{1,0:T(8,128)}, f32[256,256]{1,0:T(8,128)}) custom-call(f32[128,256]{1,0:T(8,128)} %get-tuple-element.9.subspace, f32[256,256]{1,0:T(8,128)} %get-tuple-element.10.ritz, f32[128,256]{1,0:T(8,128)} %get-tuple-element.11.residual, f32[256,256]{1,0:T(8,128)} %get-tuple-element.12.gram, ...), custom_call_target="tpu_custom_call" | custom-call | tf_op jit(solution)/shard_map/pallas_call | solution.py:474

commit v7 on v6

--- a/solution.py
+++ b/solution.py
@@ -85,7 +85,7 @@
             size = jnp.abs(block)
             dacc[pos // chips, lax.rem(pos, chips)] += jnp.sum(size.reshape(BS // 8, 8, BS), axis=0)
             return total + size
-        total = lax.fori_loop(0, n_row, fill, jnp.zeros((BS, BS), f32))
+        total = lax.fori_loop(0, n_row, fill, jnp.zeros((BS, BS), f32), unroll=4)
         rowp[0, lr, 0:8, 0:BS] = lax.dot_general(
             ones, total, (((1,), (1,)), ((), ())), precision=highest, preferred_element_type=f32)
     load.wait()

time: 165 us -> 163 us (0.988)
  Pallas kernels: 162 us -> 160 us
    pallas_call x1, Pallas kernels: 160 us -> 158 us  [fused(): pl.pallas_call(functools.partial(kernel, side, n_col, width), out_shape=(...]
where the time goes in v7:
time: 163 us
  Pallas kernels  160 us (98%)
    pallas_call x1, Pallas kernels, fused(): pl.pallas_call(functools.partial(kernel, side, n_col, width), out_shape=(...  158 us

profile of v7, /device:TPU:1, one launch (start us, length us, event | category | flops | bytes accessed | tf_op | source)
XLA Modules:
  0.0 162.7 jit_solution(15405750261945365557)
XLA Ops:
  1.3 0.8 compare_select_fusion.2
  2.1 0.7 select_reduce_fusion.table
  2.7 158.0 %shard_map.75 = (f32[128,256]{1,0:T(8,128)}, f32[256,256]{1,0:T(8,128)}, f32[128,256]{1,0:T(8,128)}, f32[256,256]{1,0:T(8,128)}, f32[2,8,128]{2,1,0:T(8,128)}) custom-call(s32[256]{0:T(256)} %select_reduce_fusion.table, bf16[128,128,128]{2,1,0:T(8,128)(2,1)} %bitcast.17, f32[128,256]{1,0:T(8,128)} %start.1), custom_call_target="tpu_custom_call" | custom-call | tf_op jit(solution)/shard_map/pallas_call | solution.py:374
  160.7 2.0 %shard_map.76 = (f32[128,256]{1,0:T(8,128)}, f32[256,256]{1,0:T(8,128)}, f32[128,256]{1,0:T(8,128)}, f32[256,256]{1,0:T(8,128)}) custom-call(f32[128,256]{1,0:T(8,128)} %get-tuple-element.9.subspace, f32[256,256]{1,0:T(8,128)} %get-tuple-element.10.ritz, f32[128,256]{1,0:T(8,128)} %get-tuple-element.11.residual, f32[256,256]{1,0:T(8,128)} %get-tuple-element.12.gram, ...), custom_call_target="tpu_custom_call" | custom-call | tf_op jit(solution)/shard_map/pallas_call | solution.py:474
